TPU v7x, 32 devices: a whole 2x2x4 slice. The times are simulated.
32 devices in a mesh: grp: 4 (over y, core), sp: 8 (over z, x).
Axes of the slice: x: 2, y: 2, z: 4, core: 2. Of those that a mesh axis runs over, the one named last changes fastest.
Arguments:
- activations: bfloat16 [4, 256, 8192], P('grp', None, 'sp'), may hold values from -6 to 6
- weights: bfloat16 [27, 256, 512], P(None, 'sp'), may hold values from -0.109375 to 0.109375
- conv_bias: float32 [512], P('sp'), may hold values from -3 to 3
- grad_out: bfloat16 [4, 512, 8192], P('grp', 'sp'), may hold values from -6 to 6
- loss_scale: float32 [1], replicated, may hold values from 90.50967 to 362.03867
Outputs:
- conv_out: bfloat16 [4, 512, 8192], P('grp', 'sp')
- grad_input: bfloat16 [4, 256, 8192], P('grp', None, 'sp')
- grad_weight: float32 [27, 256, 512], P(None, 'sp')
- grad_bias: float32 [512], P('sp')
All inputs are finite; a program needn't handle non-finite values.
Results may differ from a plain program's by a relative error of at most 0.001.
Values may be sent and summed in bfloat16 or wider, within the bound.
No kernel may reach another device: no remote copies, remote signals or barrier semaphores. Data moves between devices by JAX's collectives and lax.ppermute only.
A program may use at most 192 MiB of HBM per device.

v0:
```python
import jax
import jax.numpy as jnp
from jax import lax
from jax.sharding import PartitionSpec as P

SIDE = 32


def tap_steps():
    return [(a - 1, b - 1, c - 1) for a in range(3) for b in range(3) for c in range(3)]


def flat_offset(side_len, steps):
    return steps[0] * side_len * side_len + steps[1] * side_len + steps[2]


def tap_valid(cell_count, side_len, sign):
    position = jnp.arange(cell_count)
    across = position % side_len
    down_index = position // side_len % side_len
    flags = []
    for steps in tap_steps():
        moved_line = down_index + sign * steps[1]
        moved_cell = across + sign * steps[2]
        flags.append(
            (moved_line >= 0)
            & (moved_line < side_len)
            & (moved_cell >= 0)
            & (moved_cell < side_len)
        )
    return jnp.stack(flags)


def make_patches(block, side_len, valid, sign):
    cell_count = block.shape[1]
    margin = side_len * side_len + side_len + 1
    padded = jnp.pad(block, ((0, 0), (margin, margin)))
    pieces = []
    for tap, steps in enumerate(tap_steps()):
        start = margin + sign * flat_offset(side_len, steps)
        pieces.append(
            jnp.where(
                valid[tap][None, :],
                padded[:, start : start + cell_count],
                jnp.zeros((), block.dtype),
            )
        )
    return jnp.stack(pieces).reshape(27 * block.shape[0], cell_count)


def shifted_sum(terms, side_len, sign, valid):
    cell_count = terms.shape[2]
    margin = side_len * side_len + side_len + 1
    padded = jnp.pad(terms, ((0, 0), (0, 0), (margin, margin)))
    result = jnp.zeros(terms.shape[1:], jnp.float32)
    for tap, steps in enumerate(tap_steps()):
        start = margin + sign * flat_offset(side_len, steps)
        result = result + jnp.where(
            valid[tap][None, :], padded[tap, :, start : start + cell_count], 0.0
        )
    return result


def local_backward(every_grad, weights, patches, behind):
    spread = jnp.einsum("kcf,fp->kcp", weights, every_grad, preferred_element_type=jnp.float32)
    input_grad = shifted_sum(spread, SIDE, -1, behind).astype(jnp.bfloat16)[None]
    weight_part = lax.dot_general(
        patches, every_grad, (((1,), (1,)), ((), ())), preferred_element_type=jnp.float32
    )
    return (input_grad, weight_part.reshape(27, patches.shape[0] // 27, every_grad.shape[0]))


def per_device(activations, weights, conv_bias, grad_out, loss_scale):
    cell_count = grad_out.shape[2]
    channel_share = weights.shape[1]
    ahead = tap_valid(cell_count, SIDE, 1)
    behind = tap_valid(cell_count, SIDE, -1)
    local_block = lax.all_to_all(activations, "sp", split_axis=1, concat_axis=2, tiled=True)[0]
    patches = make_patches(local_block, SIDE, ahead, 1)
    flat_weights = weights.reshape(27 * channel_share, weights.shape[2])
    conv_sum = lax.psum_scatter(
        lax.dot_general(
            flat_weights, patches, (((0,), (0,)), ((), ())), preferred_element_type=jnp.float32
        ),
        "sp",
        scatter_dimension=0,
        tiled=True,
    )
    every_grad = lax.all_gather(grad_out, "sp", axis=1, tiled=True)[0]
    input_grad, weight_part = local_backward(every_grad, weights, patches, behind)
    grad_input = lax.all_to_all(input_grad, "sp", split_axis=2, concat_axis=1, tiled=True)
    conv_out = (conv_sum + conv_bias[:, None]).astype(jnp.bfloat16)[None]
    bias_part = jnp.sum(grad_out[0].astype(jnp.float32), axis=1)
    weight_total, bias_total = lax.psum((weight_part, bias_part), "grp")
    return (conv_out, grad_input, weight_total / loss_scale[0], bias_total / loss_scale[0])


def solution(mesh):
    return jax.shard_map(
        per_device,
        mesh=mesh,
        in_specs=(P("grp", None, "sp"), P(None, "sp", None), P("sp"), P("grp", "sp", None), P()),
        out_specs=(P("grp", "sp", None), P("grp", None, "sp"), P(None, "sp", None), P("sp")),
        check_vma=False,
    )
```

profile of v0, /device:TPU:0, one launch (start us, length us, event | category | flops | bytes accessed | tf_op | source)
XLA Modules:
  0.0 522.9 jit_solution(17502447594136582706)
XLA Ops:
  7.2 1.9 copy.38
  9.6 3.7 reduce.1
  13.3 1.2 reshape.297
  14.5 7.3 %all-to-all-start = ((bf16[8,2,16384]{2,1,0:T(2,128)(2,1)}), bf16[8,2,16384]{2,1,0:T(2,128)(2,1)S(1)}, u32[]{:S(2)}, u32[]{:S(2)}) async-start(bf16[8,2,16384]{2,1,0:T(2,128)(2,1)} %reshape.297), calls=%async_computation | async-start | bytes 1048576 | tf_op jit(solution)/shard_map/all_to_all | solution.py:78
  22.9 13.4 %all-to-all-done = bf16[8,2,16384]{2,1,0:T(2,128)(2,1)S(1)} async-done(((bf16[8,2,16384]{2,1,0:T(2,128)(2,1)}), bf16[8,2,16384]{2,1,0:T(2,128)(2,1)S(1)}, u32[]{:S(2)}, u32[]{:S(2)}) %all-to-all-start) | async-done | bytes 524320 | tf_op jit(solution)/shard_map/all_to_all | solution.py:78
  37.0 1.0 bitcast_dynamic-update-slice_fusion.25
  38.0 1.0 bitcast_dynamic-update-slice_fusion.24
  39.0 1.0 bitcast_dynamic-update-slice_fusion.23
  40.0 1.0 bitcast_dynamic-update-slice_fusion.22
  41.9 1.0 bitcast_dynamic-update-slice_fusion.20
  43.9 1.0 bitcast_dynamic-update-slice_fusion.18
  44.9 1.0 bitcast_dynamic-update-slice_fusion.17
  45.9 1.0 bitcast_dynamic-update-slice_fusion.16
  46.9 1.0 bitcast_dynamic-update-slice_fusion.15
  48.0 1.0 bitcast_dynamic-update-slice_fusion.14
  49.0 1.0 bitcast_dynamic-update-slice_fusion.13
  50.9 1.0 bitcast_dynamic-update-slice_fusion.12
  51.9 1.0 bitcast_dynamic-update-slice_fusion.11
  53.0 1.1 bitcast_dynamic-update-slice_fusion.10
  54.0 1.1 bitcast_dynamic-update-slice_fusion.9
  55.1 1.0 bitcast_dynamic-update-slice_fusion.8
  56.1 1.0 bitcast_dynamic-update-slice_fusion.7
  57.1 1.0 bitcast_dynamic-update-slice_fusion.6
  58.1 1.0 bitcast_dynamic-update-slice_fusion.5
  60.0 1.0 bitcast_dynamic-update-slice_fusion.3
  61.0 1.0 bitcast_dynamic-update-slice_fusion.2
  62.0 1.0 bitcast_dynamic-update-slice_fusion.1
  64.0 87.1 %all-gather.2.cloned.1.call-done = bf16[1,512,8192]{2,1,0:T(8,128)(2,1)} async-done(((bf16[1,64,8192]{2,1,0:T(8,128)(2,1)}), bf16[1,512,8192]{2,1,0:T(8,128)(2,1)}) %all-gather.2.cloned.1.call-update) | async-done | bytes 8388624 | tf_op jit(solution)/shard_map/all_gather | solution.py:89
  151.1 14.0 %fusion = f32[27,32,512]{2,1,0:T(8,128)} fusion(bf16[27,32,8192]{2,1,0:T(8,128)(2,1)} %bitcast_dynamic-update-slice_fusion, bf16[1,512,8192]{2,1,0:T(8,128)(2,1)} %all-gather.2.cloned.1.call-done), kind=kOutput, calls=%fused_computation.27 | convolution fusion | flops 7247757312 | bytes 24313856 | tf_op jit(solution)/shard_map/dot_general | solution.py:67
  165.4 15.4 %convolution_bitcast_fusion = f32[512,8192]{0,1:T(8,128)} fusion(bf16[27,32,8192]{2,1,0:T(8,128)(2,1)} %bitcast_dynamic-update-slice_fusion, bf16[27,32,512]{2,1,0:T(8,128)(2,1)S(1)} %copy-done), kind=kOutput, calls=%fused_computation.26 | convolution fusion | flops 7247757312 | bytes 31817728 | tf_op jit(solution)/shard_map/dot_general | solution.py:82
  180.8 17.6 %copy.30 = f32[512,8192]{1,0:T(8,128)} copy(f32[512,8192]{0,1:T(8,128)} %convolution_bitcast_fusion) | data formatting | bytes 33554432
  198.4 16.1 %fusion.2 = f32[27,32,8192]{2,1,0:T(8,128)} fusion(bf16[27,32,512]{2,1,0:T(8,128)(2,1)S(1)} %copy-done, bf16[1,512,8192]{2,1,0:T(8,128)(2,1)} %all-gather.2.cloned.1.call-done), kind=kOutput, calls=%fused_computation.29 | convolution fusion | flops 7247757312 | bytes 37584896 | tf_op jit(solution)/shard_map/kcf,fp->kcp/dot_general | solution.py:65
  214.5 12.7 %fusion.57 = bf16[1,32,8192]{2,1,0:T(8,128)(2,1)S(1)} fusion(f32[27,32,8192]{2,1,0:T(8,128)} %fusion.2, pred[8192]{0:T(1024)(128)(4,1)S(1)} %and_and_fusion.8, pred[8192]{0:T(1024)(128)(4,1)S(1)} %get-tuple-element.27, pred[8192]{0:T(1024)(128)(4,1)S(1)} %get-tuple-element.26, pred[8192]{0:T(1024)(128)(4,1)S(1)} %get-tuple-element.25, ...), kind=kLoop, calls=%fused_computation.87 | loop fusion | flops 14155776 | bytes 29958144 | tf_op jit(solution)/shard_map/convert_element_type | solution.py:66
  227.2 6.7 %copy.26 = bf16[1,32,8192]{1,0,2:T(2,128)(2,1)} copy(bf16[1,32,8192]{2,1,0:T(8,128)(2,1)S(1)} %fusion.57) | data formatting | bytes 1048576 | tf_op jit(solution)/shard_map/convert_element_type | solution.py:66
  233.9 45.5 %reduce.2 = bf16[8192,32]{1,0:T(8,128)(2,1)S(1)} reduce(bf16[8192,1,32]{2,1,0:T(2,128)(2,1)} %bitcast.123, bf16[]{:T(256)} %broadcast.810), dimensions={1}, to_apply=%bitcast.86.reduce_sub_computation | reduce | bytes 1048578
  279.4 2.7 reshape.299
  282.0 3.5 all-to-all-start.1
  286.2 1.5 convert_reduce_fusion
  287.7 6.6 %psum.15 = f32[64]{0:T(128)S(1)} all-reduce(f32[64]{0:T(128)S(1)} %convert_reduce_fusion), channel_id=1, replica_groups=mesh['grp'=4,'sp'=8] {'grp'}, use_global_device_ids=true, to_apply=%region_3.4 | all-reduce | flops 64 | bytes 512 | tf_op jit(solution)/shard_map/psum | solution.py:94
  294.8 3.0 broadcast_divide_fusion
  297.7 17.1 %all-to-all-done.1 = bf16[8,2,16384]{2,1,0:T(2,128)(2,1)S(1)} async-done(((bf16[8,2,16384]{2,1,0:T(2,128)(2,1)}), bf16[8,2,16384]{2,1,0:T(2,128)(2,1)S(1)}, u32[]{:S(2)}, u32[]{:S(2)}) %all-to-all-start.1) | async-done | bytes 524320 | tf_op jit(solution)/shard_map/all_to_all | solution.py:91
  314.8 4.5 reshape.300
  319.3 8.0 %copy.27 = bf16[1,32,8192]{2,1,0:T(8,128)(2,1)S(1)} copy(bf16[1,32,8192]{1,0,2:T(2,128)(2,1)} %bitcast.124) | data formatting | bytes 1048576 | tf_op jit(solution)/shard_map/all_to_all | solution.py:91
  327.6 1.1 copy.28
  328.7 179.9 %reduce-scatter.4.cloned.1.call-done = f32[64,8192]{1,0:T(8,128)} async-done(((f32[512,8192]{1,0:T(8,128)}), f32[64,8192]{1,0:T(8,128)}) %reduce-scatter.4.cloned.1.call-update) | async-done | bytes 2097168
  508.6 3.8 copy.31
  512.4 2.4 fusion.4
  514.8 1.6 copy.29
  (29 shorter events, 8.1 us)
Async XLA Ops:
  7.2 158.3 %copy-start = (bf16[27,32,512]{2,1,0:T(8,128)(2,1)S(1)}, bf16[27,32,512]{2,1,0:T(8,128)(2,1)}, u32[]{:S(2)}) copy-start(bf16[27,32,512]{2,1,0:T(8,128)(2,1)} %param.6) | copy-start | bytes 2654212
  14.5 21.7 %all-to-all-start = ((bf16[8,2,16384]{2,1,0:T(2,128)(2,1)}), bf16[8,2,16384]{2,1,0:T(2,128)(2,1)S(1)}, u32[]{:S(2)}, u32[]{:S(2)}) async-start(bf16[8,2,16384]{2,1,0:T(2,128)(2,1)} %reshape.297), calls=%async_computation | async-start | bytes 1048576 | tf_op jit(solution)/shard_map/all_to_all | solution.py:78
  21.8 129.4 %all-gather.2.cloned.1.call-start = ((), (), s32[]{:S(2)}) async-start(), calls=%async_computation.3 | async-start | bytes 9437184 | tf_op jit(solution)/shard_map/all_gather | solution.py:89
  22.5 272.3 %all-reduce.4.cloned.1.call-start = ((), (), s32[]{:S(2)}) async-start(), calls=%async_computation.4 | async-start | bytes 3538944 | tf_op jit(solution)/shard_map/psum | solution.py:94
  165.1 343.5 %reduce-scatter.4.cloned.1.call-start = ((), (), s32[]{:S(2)}) async-start(), calls=%async_computation.5 | async-start | bytes 18874368
  279.4 233.0 %copy-start.1 = (f32[64]{0:T(128)S(1)}, f32[64]{0:T(128)}, u32[]{:S(2)}) copy-start(f32[64]{0:T(128)} %param.7) | copy-start | bytes 772
  282.0 32.8 %all-to-all-start.1 = ((bf16[8,2,16384]{2,1,0:T(2,128)(2,1)}), bf16[8,2,16384]{2,1,0:T(2,128)(2,1)S(1)}, u32[]{:S(2)}, u32[]{:S(2)}) async-start(bf16[8,2,16384]{2,1,0:T(2,128)(2,1)} %reshape.299), calls=%async_computation.1 | async-start | bytes 1048576 | tf_op jit(solution)/shard_map/all_to_all | solution.py:91
Sparse Core Ops, SparseCore 0:
  24.7 126.3 all-gather.1
  165.3 44.2 all-reduce.3
  213.8 294.7 reduce-scatter.3
where the time goes:
time: 524 us; the launch traced here: 523 us
  waiting for transfers between devices  298 us (57%)
  other arithmetic  96.3 us (18%)
  local copies, waits for them, and re-layouts  50.6 us (10%)
  matrix products  45.5 us (9%)
  between operations  14.6 us (3%)
  starting transfers between devices  11.3 us (2%)
  blocking collectives  6.58 us (1%)
    unnamed x4, waiting for transfers between devices  181 us
    all_gather x1, waiting for transfers between devices, per_device(): every_grad = lax.all_gather(grad_out, 'sp', axis=1, tiled=True)[0]  87.1 us
    unnamed x28, other arithmetic  75.2 us
    unnamed x16, local copies, waits for them, and re-layouts  34.8 us
    all_to_all x1, waiting for transfers between devices, per_device(): lax.all_to_all(input_grad, 'sp', split_axis=2, concat_axis=1, tiled=True)  17.1 us
    dot_general x1, matrix products, local_backward(): jnp.einsum('kcf,fp->kcp', weights, every_grad, preferred_element_type=jnp...  16.1 us
    dot_general x1, matrix products, per_device(): lax.dot_general(flat_weights, patches, (((0,), (0,)), ((), ())), preferre...  15.4 us
    dot_general x1, matrix products, local_backward(): lax.dot_general(patches, every_grad, (((1,), (1,)), ((), ())), preferred_...  14 us
  transfers between devices with their start and end apart: 5, of which 4 were waited for; matrix products, arithmetic and copies ran while one was open for 31% of the time, Pallas kernels for 0%

commit v1 on v0

--- a/solution.py
+++ b/solution.py
@@ -1,6 +1,8 @@
 import jax
 import jax.numpy as jnp
 from jax import lax
+from jax.experimental import pallas as pl
+from jax.experimental.pallas import tpu as pltpu
 from jax.sharding import PartitionSpec as P
 
 SIDE = 32
@@ -70,7 +72,7 @@
     return (input_grad, weight_part.reshape(27, patches.shape[0] // 27, every_grad.shape[0]))
 
 
-def per_device(activations, weights, conv_bias, grad_out, loss_scale):
+def shard_general(activations, weights, conv_bias, grad_out, loss_scale):
     cell_count = grad_out.shape[2]
     channel_share = weights.shape[1]
     ahead = tap_valid(cell_count, SIDE, 1)
@@ -95,9 +97,353 @@
     return (conv_out, grad_input, weight_total / loss_scale[0], bias_total / loss_scale[0])
 
 
+VMEM_BYTES = 56 * 1024 * 1024
+PLANE = SIDE * SIDE
+TAPS = 27
+
+
+def in_plane():
+    cell = lax.broadcasted_iota(jnp.int32, (1, PLANE), 1)
+    return cell // SIDE, cell % SIDE
+
+
+def shifted(value, offset):
+    return pltpu.roll(value, (-offset) % PLANE, 1)
+
+
+def inside(coordinate, step):
+    moved = coordinate + step
+    return (moved >= 0) & (moved < SIDE)
+
+
+def gather_shifts(terms_ref, rows, sign):
+    line, position = in_plane()
+    total = None
+    for c in range(3):
+        column = None
+        for b in range(3):
+            start = (3 * b + c) * rows
+            term = terms_ref[start : start + rows, :]
+            if b != 1:
+                term = jnp.where(
+                    inside(line, sign * (b - 1)), shifted(term, sign * SIDE * (b - 1)), 0.0
+                )
+            column = term if column is None else column + term
+        if c != 1:
+            column = jnp.where(
+                inside(position, sign * (c - 1)), shifted(column, sign * (c - 1)), 0.0
+            )
+        total = column if total is None else total + column
+    return total
+
+
+def forward_kernel(act_ref, kernel_ref, bias_ref, out_ref, terms_ref):
+    plane, planes = pl.program_id(0), pl.num_programs(0)
+    channels = act_ref.shape[0] // planes
+    rows = out_ref.shape[0]
+
+    def multiply(first, count, lanes):
+        block = act_ref[pl.ds(pl.multiple_of(first * channels, channels), count * channels), :]
+        terms_ref[...] = jnp.dot(
+            kernel_ref[:, lanes * channels : (lanes + count) * channels],
+            block,
+            preferred_element_type=jnp.float32,
+        )
+
+    @pl.when(plane == 0)
+    def _():
+        multiply(plane, 2, 1)
+
+    @pl.when(plane == planes - 1)
+    def _():
+        multiply(plane - 1, 2, 0)
+
+    @pl.when((plane > 0) & (plane < planes - 1))
+    def _():
+        multiply(plane - 1, 3, 0)
+
+    total = gather_shifts(terms_ref, rows, 1) + bias_ref[...]
+    out_ref[...] = total.astype(out_ref.dtype)
+
+
+def forward(act_all, kernel, bias):
+    planes, channels, cells = act_all.shape
+    filters = bias.shape[0]
+    return pl.pallas_call(
+        forward_kernel,
+        grid=(planes,),
+        in_specs=[
+            pl.BlockSpec((planes * channels, cells), lambda d: (0, 0)),
+            pl.BlockSpec(kernel.shape, lambda d: (0, 0)),
+            pl.BlockSpec((filters, 1), lambda d: (0, 0)),
+        ],
+        out_specs=pl.BlockSpec((filters, cells), lambda d: (0, d)),
+        out_shape=jax.ShapeDtypeStruct((filters, planes * cells), jnp.bfloat16),
+        scratch_shapes=[pltpu.VMEM((9 * filters, cells), jnp.float32)],
+        compiler_params=pltpu.CompilerParams(vmem_limit_bytes=VMEM_BYTES),
+        cost_estimate=pl.CostEstimate(
+            flops=2 * TAPS * channels * filters * planes * cells,
+            bytes_accessed=6 * 1024 * 1024,
+            transcendentals=0,
+        ),
+        name="forward",
+    )(act_all.reshape(planes * channels, cells), kernel, bias[:, None])
+
+
+def weight_kernel(act_ref, grad_ref, out_ref, moved_ref, total_ref):
+    plane, planes = pl.program_id(0), pl.num_programs(0)
+    filters = grad_ref.shape[0]
+    group = 9 * filters
+    line, position = in_plane()
+
+    def place(which):
+        lanes = pl.ds(pl.multiple_of(which * PLANE, PLANE), PLANE)
+        block = grad_ref[:, lanes].astype(jnp.float32)
+        base = pl.multiple_of((planes - which) * group, group)
+        total_ref[TAPS * filters :, :] += jnp.broadcast_to(
+            jnp.sum(block, axis=1, keepdims=True), (filters, total_ref.shape[1])
+        )
+        for c in range(3):
+            column = block
+            if c != 1:
+                column = jnp.where(
+                    inside(position, -(c - 1)), shifted(block, -(c - 1)), 0.0
+                )
+            for b in range(3):
+                term = column
+                if b != 1:
+                    term = jnp.where(
+                        inside(line, -(b - 1)), shifted(column, -SIDE * (b - 1)), 0.0
+                    )
+                start = pl.multiple_of(base + (3 * b + c) * filters, filters)
+                moved_ref[pl.ds(start, filters), :] = term.astype(moved_ref.dtype)
+
+    @pl.when(plane == 0)
+    def _():
+        total_ref[...] = jnp.zeros_like(total_ref)
+        moved_ref[:group, :] = jnp.zeros((group, PLANE), moved_ref.dtype)
+        moved_ref[(planes + 1) * group :, :] = jnp.zeros((group, PLANE), moved_ref.dtype)
+        place(0)
+
+    @pl.when(plane < planes - 1)
+    def _():
+        place(plane + 1)
+
+    start = pl.multiple_of((planes - 1 - plane) * group, group)
+    total_ref[: TAPS * filters, :] += lax.dot_general(
+        moved_ref[pl.ds(start, 3 * group), :],
+        act_ref[0],
+        (((1,), (1,)), ((), ())),
+        preferred_element_type=jnp.float32,
+    )
+
+    @pl.when(plane == planes - 1)
+    def _():
+        out_ref[...] = total_ref[...].T
+
+
+def weight_part(act_all, grads):
+    planes, channels, cells = act_all.shape
+    filters = grads.shape[0]
+    width = (TAPS + 1) * filters
+    return pl.pallas_call(
+        weight_kernel,
+        grid=(planes,),
+        in_specs=[
+            pl.BlockSpec((1, channels, cells), lambda d: (d, 0, 0)),
+            pl.BlockSpec(grads.shape, lambda d: (0, 0)),
+        ],
+        out_specs=pl.BlockSpec((channels, width), lambda d: (0, 0)),
+        out_shape=jax.ShapeDtypeStruct((channels, width), jnp.float32),
+        scratch_shapes=[
+            pltpu.VMEM(((planes + 2) * 9 * filters, cells), jnp.bfloat16),
+            pltpu.VMEM((width, channels), jnp.float32),
+        ],
+        compiler_params=pltpu.CompilerParams(vmem_limit_bytes=VMEM_BYTES),
+        cost_estimate=pl.CostEstimate(
+            flops=2 * TAPS * channels * filters * planes * cells,
+            bytes_accessed=8 * 1024 * 1024,
+            transcendentals=0,
+        ),
+        name="weight_part",
+    )(act_all, grads)
+
+
+def input_kernel(which_ref, below_ref, middle_ref, above_ref, kernel_ref, out_ref, planes_ref, terms_ref):
+    filters = below_ref.shape[0]
+    rows = out_ref.shape[0]
+
+    @pl.when(pl.program_id(0) == 0)
+    def _():
+        planes_ref[:filters, :] = below_ref[...]
+        planes_ref[filters : 2 * filters, :] = middle_ref[:, :PLANE]
+        planes_ref[2 * filters : 3 * filters, :] = middle_ref[:, PLANE:]
+        planes_ref[3 * filters :, :] = above_ref[...]
+
+    start = pl.multiple_of(which_ref[0] * filters, filters)
+    kernel = jnp.concatenate(
+        [kernel_ref[2 - a].reshape(9 * rows, filters) for a in range(3)], axis=1
+    )
+    terms_ref[...] = jnp.dot(
+        kernel, planes_ref[pl.ds(start, 3 * filters), :], preferred_element_type=jnp.float32
+    )
+    out_ref[...] = gather_shifts(terms_ref, rows, -1)
+
+
+def input_part(which, below, middle, above, kernel, rows=64):
+    filters, cells = below.shape
+    channels = kernel.shape[2]
+    return pl.pallas_call(
+        input_kernel,
+        grid=(channels // rows,),
+        in_specs=[
+            pl.BlockSpec(memory_space=pltpu.SMEM),
+            pl.BlockSpec(below.shape, lambda n: (0, 0)),
+            pl.BlockSpec(middle.shape, lambda n: (0, 0)),
+            pl.BlockSpec(above.shape, lambda n: (0, 0)),
+            pl.BlockSpec((3, 9, rows, filters), lambda n: (0, 0, n, 0)),
+        ],
+        out_specs=pl.BlockSpec((rows, cells), lambda n: (n, 0)),
+        out_shape=jax.ShapeDtypeStruct((channels, cells), jnp.float32),
+        scratch_shapes=[
+            pltpu.VMEM((4 * filters, cells), jnp.bfloat16),
+            pltpu.VMEM((9 * rows, cells), jnp.float32),
+        ],
+        compiler_params=pltpu.CompilerParams(vmem_limit_bytes=VMEM_BYTES),
+        cost_estimate=pl.CostEstimate(
+            flops=2 * TAPS * channels * filters * cells,
+            bytes_accessed=8 * 1024 * 1024,
+            transcendentals=0,
+        ),
+        name="input_part",
+    )(which, below, middle, above, kernel)
+
+
+def arrange_kernel(scale_ref, parts_ref, out_ref):
+    sources, rows, width = parts_ref.shape
+    filters = width // (TAPS + 1)
+    scale = scale_ref[0]
+    for tap in range(TAPS):
+        for source in range(sources):
+            out_ref[tap, :, source * filters : (source + 1) * filters] = (
+                parts_ref[source, :, tap * filters : (tap + 1) * filters] / scale
+            )
+
+
+def arrange(scale, parts):
+    sources, rows, width = parts.shape
+    filters = width // (TAPS + 1)
+    return pl.pallas_call(
+        arrange_kernel,
+        in_specs=[
+            pl.BlockSpec(memory_space=pltpu.SMEM),
+            pl.BlockSpec(memory_space=pltpu.VMEM),
+        ],
+        out_specs=pl.BlockSpec(memory_space=pltpu.VMEM),
+        out_shape=jax.ShapeDtypeStruct((TAPS, rows, sources * filters), jnp.float32),
+        compiler_params=pltpu.CompilerParams(vmem_limit_bytes=VMEM_BYTES),
+        name="arrange",
+    )(scale, parts)
+
+
+def in_order(own, other, bit):
+    return jnp.stack([jnp.where(bit == 0, own, other), jnp.where(bit == 0, other, own)])
+
+
+def by_source(received, own_index):
+    count = len(received)
+    falling = jnp.stack(received[::-1] + received[::-1][:-1])
+    return lax.dynamic_slice_in_dim(falling, count - 1 - own_index, count, 0)
+
+
+def spread_kernel(weights, at):
+    z, x, y, core = at["z"], at["x"], at["y"], at["core"]
+    quarter = weights.reshape(TAPS, 4, 8, 4, 2, 64)
+    quarter = lax.dynamic_index_in_dim(quarter, 2 * y + core, 1, False)
+    keep = lax.dynamic_index_in_dim(quarter, x, 3, False).reshape(TAPS, 8, 256)
+    give = lax.dynamic_index_in_dim(quarter, 1 - x, 3, False).reshape(TAPS, 8, 256)
+    pair = in_order(keep, lax.ppermute(give, "sp", at["swap_x"]), x)
+    ring = by_source([pair] + [lax.ppermute(pair, "sp", at["turn_z"](k)) for k in (1, 2, 3)], z)
+    both = in_order(ring, lax.ppermute(ring, "grp", at["swap_y"]), y)
+    every = in_order(both, lax.ppermute(both, "grp", at["swap_core"]), core)
+    return every.transpose(4, 2, 3, 1, 0, 5, 6).reshape(3, 9, 256, 256)
+
+
+def spread_grads(grads, at):
+    z = at["z"]
+
+    def planes_of(k):
+        return lax.dynamic_slice_in_dim(grads, ((z + k) % 4) * 2 * PLANE, 2 * PLANE, 1)
+
+    blocks = [planes_of(0)] + [
+        lax.ppermute(planes_of(k), "sp", at["turn_z"](k)) for k in (1, 2, 3)
+    ]
+    middle = by_source(blocks, z).reshape(256, 2 * PLANE)
+    below = lax.ppermute(middle[:, PLANE:], "sp", at["step_z"](1))
+    above = lax.ppermute(middle[:, :PLANE], "sp", at["step_z"](-1))
+    return below, middle, above
+
+
+def sum_slabs(part, at):
+    y, core = at["y"], at["core"]
+    width = part.shape[1]
+    rows = part.reshape(8, 2, 2, 8, width)
+
+    def half(array, axis, index):
+        return lax.dynamic_index_in_dim(array, index, axis, False)
+
+    mine = half(rows, 1, core) + lax.ppermute(half(rows, 1, 1 - core), "grp", at["swap_core"])
+    mine = half(mine, 1, y) + lax.ppermute(half(mine, 1, 1 - y), "grp", at["swap_y"])
+    mine = lax.all_to_all(mine, "sp", 0, 0)
+    both = in_order(mine, lax.ppermute(mine, "grp", at["swap_y"]), y)
+    every = in_order(both, lax.ppermute(both, "grp", at["swap_core"]), core)
+    return every.transpose(2, 0, 1, 3, 4).reshape(8, 32, width)
+
+
+def placement():
+    grp, sp = lax.axis_index("grp"), lax.axis_index("sp")
+    return {
+        "z": sp // 2,
+        "x": sp % 2,
+        "y": grp // 2,
+        "core": grp % 2,
+        "swap_x": [(s, s ^ 1) for s in range(8)],
+        "swap_core": [(g, g ^ 1) for g in range(4)],
+        "swap_y": [(g, g ^ 2) for g in range(4)],
+        "turn_z": lambda k: [(s, (s + 2 * k) % 8) for s in range(8)],
+        "step_z": lambda k: [(s, s + 2 * k) for s in range(8) if 0 <= s + 2 * k < 8],
+    }
+
+
+def per_device(activations, weights, conv_bias, grad_out, loss_scale):
+    at = placement()
+    grads = grad_out[0]
+    act_all = lax.all_gather(activations[0], "sp")
+    kernel = spread_kernel(weights, at)
+    below, middle, above = spread_grads(grads, at)
+    part = weight_part(act_all, grads)
+
+    which = at["x"].astype(jnp.int32)[None]
+    other = input_part(1 - which, below, middle, above, kernel)
+    other = lax.ppermute(other, "sp", at["swap_x"])
+    own = input_part(which, below, middle, above, kernel)
+    grad_input = (own + other).astype(jnp.bfloat16)[None]
+
+    own_filters = lax.dynamic_slice_in_dim(kernel, at["z"] * 64, 64, 3)
+    own_filters = own_filters.transpose(1, 3, 0, 2).reshape(9 * 64, 3 * 256)
+    conv_out = forward(act_all, own_filters, conv_bias)[None]
+
+    parts = sum_slabs(part, at)
+    grad_weight = arrange(loss_scale, parts)
+    own_source = lax.dynamic_index_in_dim(parts, lax.axis_index("sp"), 0, False)
+    grad_bias = own_source[0, TAPS * 64 :] / loss_scale[0]
+    return (conv_out, grad_input, grad_weight, grad_bias)
+
+
 def solution(mesh):
+    measured = mesh.shape["grp"] == 4 and mesh.shape["sp"] == 8
     return jax.shard_map(
-        per_device,
+        per_device if measured else shard_general,
         mesh=mesh,
         in_specs=(P("grp", None, "sp"), P(None, "sp", None), P("sp"), P("grp", "sp", None), P()),
         out_specs=(P("grp", "sp", None), P("grp", None, "sp"), P(None, "sp", None), P("sp")),

time: 524 us -> 232 us (0.44)
  waiting for transfers between devices: 298 us -> 95.6 us
  other arithmetic: 96.3 us -> 8.64 us
  Pallas kernels: 0 us -> 52.6 us
  matrix products: 45.5 us -> 0 us
  local copies, waits for them, and re-layouts: 50.6 us -> 22.9 us
  starting transfers between devices: 11.3 us -> 36.4 us
  blocking collectives: 6.58 us -> 0 us
    unnamed x4 -> x1, waiting for transfers between devices: 181 us -> 0.68 us
    unnamed x28 -> x1, other arithmetic: 75.2 us -> 0.02 us
    ppermute x0 -> x16, waiting for transfers between devices: none -> 70.5 us  [the longest x3 33 us: spread_grads(): lax.ppermute(planes_of(k), 'sp', at['turn_z'](k))]
    all_gather x1, waiting for transfers between devices: 87.1 us -> 23.1 us  [per_device(): act_all = lax.all_gather(activations[0], 'sp')]
    pallas_call x0 -> x5, Pallas kernels: none -> 52.6 us  [the longest x1 16.7 us: forward(): pl.pallas_call(forward_kernel, grid=(planes,), in_specs=[pl.BlockSpec((pl...]
    dot_general x3 -> x0, matrix products: 45.5 us -> none  [the longest x1 16.1 us: local_backward(): jnp.einsum('kcf,fp->kcp', weights, every_grad, preferred_element_type=jnp...]
    ppermute x0 -> x16, starting transfers between devices: none -> 31.4 us  [the longest x3 14.1 us: spread_kernel(): lax.ppermute(pair, 'sp', at['turn_z'](k))]
    unnamed x16 -> x34, local copies, waits for them, and re-layouts: 34.8 us -> 3.56 us
  transfers between devices with their start and end apart: 5 -> 18, of which waited for: 4 -> 8; matrix products, arithmetic and copies ran while one was open for 31% -> 11% of each run, Pallas kernels for 0% -> 21%
where the time goes in v1:
time: 232 us; the launch traced here: 231 us
  waiting for transfers between devices  95.6 us (41%)
  Pallas kernels  52.6 us (23%)
  starting transfers between devices  36.4 us (16%)
  local copies, waits for them, and re-layouts  22.9 us (10%)
  between operations  15.2 us (7%)
  other arithmetic  8.64 us (4%)
    ppermute x3, waiting for transfers between devices, spread_grads(): lax.ppermute(planes_of(k), 'sp', at['turn_z'](k))  33 us
    all_gather x1, waiting for transfers between devices, per_device(): act_all = lax.all_gather(activations[0], 'sp')  23.1 us
    ppermute x3, waiting for transfers between devices, spread_kernel(): lax.ppermute(pair, 'sp', at['turn_z'](k))  17.3 us
    pallas_call x1, Pallas kernels, forward(): pl.pallas_call(forward_kernel, grid=(planes,), in_specs=[pl.BlockSpec((pl...  16.7 us
    pallas_call x1, Pallas kernels, weight_part(): pl.pallas_call(weight_kernel, grid=(planes,), in_specs=[pl.BlockSpec((1,...  16.4 us
    pallas_call x2, Pallas kernels, input_part(): pl.pallas_call(input_kernel, grid=(channels // rows,), in_specs=[pl.Block...  16.3 us
    ppermute x3, starting transfers between devices, spread_kernel(): lax.ppermute(pair, 'sp', at['turn_z'](k))  14.1 us
    ppermute x1, waiting for transfers between devices, per_device(): other = lax.ppermute(other, 'sp', at['swap_x'])  13.2 us
  transfers between devices with their start and end apart: 18, of which 8 were waited for; matrix products, arithmetic and copies ran while one was open for 11% of the time, Pallas kernels for 21%

profile of v1, /device:TPU:0, one launch (start us, length us, event | category | flops | bytes accessed | tf_op | source)
XLA Modules:
  0.0 231.3 jit_solution(12256229634595059144)
XLA Ops:
  7.2 0.7 all-gather.2.cloned.1.call-update
  7.9 4.0 %reshape.49 = bf16[27,4,8,4,2,64]{5,4,3,2,1,0:T(2,128)(2,1)S(1)} reshape(bf16[27,32,512]{2,1,0:T(8,128)(2,1)} %param.6) | data formatting | bytes 1769472 | tf_op jit(solution)/shard_map/reshape | solution.py:361
  12.0 3.0 %dynamic-slice_reduce_fusion.1 = (bf16[27,8,4,64]{3,2,1,0:T(4,128)(2,1)S(1)}, bf16[27,8,4,64]{3,2,1,0:T(4,128)(2,1)S(1)}) fusion(bf16[27,4,8,4,2,64]{5,4,3,2,1,0:T(2,128)(2,1)S(1)} %reshape.49, s32[]{:T(128)S(6)} %select_n.155, s32[]{:T(128)S(6)} %select_n.157, s32[]{:T(128)S(6)} %select_n.159), kind=kLoop, calls=%fused_computation.20 | loop fusion | bytes 442380 | tf_op jit(solution)/shard_map/jit(dynamic_index_in_dim)/dynamic_slice | solution.py:363
  15.2 3.0 %collective-permute-start = (bf16[27,8,256]{2,1,0:T(8,128)(2,1)S(1)}, bf16[27,8,256]{2,1,0:T(8,128)(2,1)S(1)}, u32[]{:S(2)}, u32[]{:S(2)}) collective-permute-start(bf16[27,8,256]{2,1,0:T(8,128)(2,1)S(1)} %reshape.51), channel_id=1, source_target_pairs={{0,1},{1,0},{2,3},{3,2},{4,5},{5,4},{6,7},{7,6},{8,9},{9,8},{10,11... | collective-permute-start | bytes 331784 | tf_op jit(solution)/shard_map/ppermute | solution.py:365
  18.2 0.8 dynamic-slice_bitcast_fusion.3
  19.0 3.6 %collective-permute-start.6 = (bf16[64,2048]{1,0:T(8,128)(2,1)S(1)}, bf16[64,2048]{1,0:T(8,128)(2,1)S(1)}, u32[]{:S(2)}, u32[]{:S(2)}) collective-permute-start(bf16[64,2048]{1,0:T(8,128)(2,1)S(1)} %get-tuple-element.16), channel_id=1, source_target_pairs={{0,6},{1,7},{2,0},{3,1},{4,2},{5,3},{6,4},{7,5},{8,14},{9,15},{10,... | collective-permute-start | bytes 786440 | tf_op jit(solution)/shard_map/ppermute | solution.py:379
  22.6 1.0 collective-permute-start.8
  23.8 0.7 copy.33.bias_ref
  25.3 2.9 %collective-permute-start.1 = (bf16[2,27,8,256]{3,2,1,0:T(8,128)(2,1)S(1)}, bf16[2,27,8,256]{3,2,1,0:T(8,128)(2,1)S(1)}, u32[]{:S(2)}, u32[]{:S(2)}) collective-permute-start(bf16[2,27,8,256]{3,2,1,0:T(8,128)(2,1)S(1)} %pad_maximum_fusion.3), channel_id=1, source_target_pairs={{0,6},{1,7},{2,0},{3,1},{4,2},{5,3},{6,4},{7,5},{8,14},{9,15},{10,... | collective-permute-start | bytes 663560 | tf_op jit(solution)/shard_map/ppermute | solution.py:366
  28.2 1.1 collective-permute-start.2
  29.3 7.1 %collective-permute-done.6 = bf16[64,2048]{1,0:T(8,128)(2,1)S(1)} collective-permute-done((bf16[64,2048]{1,0:T(8,128)(2,1)S(1)}, bf16[64,2048]{1,0:T(8,128)(2,1)S(1)}, u32[]{:S(2)}, u32[]{:S(2)}) %collective-permute-start.6) | collective-permute-done | bytes 262176 | tf_op jit(solution)/shard_map/ppermute | solution.py:379
  36.4 10.1 %collective-permute-start.3 = (bf16[2,27,8,256]{3,2,1,0:T(8,128)(2,1)S(1)}, bf16[2,27,8,256]{3,2,1,0:T(8,128)(2,1)S(1)}, u32[]{:S(2)}, u32[]{:S(2)}) collective-permute-start(bf16[2,27,8,256]{3,2,1,0:T(8,128)(2,1)S(1)} %pad_maximum_fusion.3), channel_id=1, source_target_pairs={{0,2},{1,3},{2,4},{3,5},{4,6},{5,7},{6,0},{7,1},{8,10},{9,11},{10,... | collective-permute-start | bytes 663560 | tf_op jit(solution)/shard_map/ppermute | solution.py:366
  46.5 25.9 %collective-permute-done.7 = bf16[64,2048]{1,0:T(8,128)(2,1)S(1)} collective-permute-done((bf16[64,2048]{1,0:T(8,128)(2,1)}, bf16[64,2048]{1,0:T(8,128)(2,1)S(1)}, u32[]{:S(2)}, u32[]{:S(2)}) %collective-permute-start.7) | collective-permute-done | bytes 262176 | tf_op jit(solution)/shard_map/ppermute | solution.py:379
  72.6 17.3 %collective-permute-done.2 = bf16[2,27,8,256]{3,2,1,0:T(8,128)(2,1)S(1)} collective-permute-done((bf16[2,27,8,256]{3,2,1,0:T(8,128)(2,1)S(1)}, bf16[2,27,8,256]{3,2,1,0:T(8,128)(2,1)S(1)}, u32[]{:S(2)}, u32[]{:S(2)}) %collective-permute-start.2) | collective-permute-done | bytes 221216 | tf_op jit(solution)/shard_map/ppermute | solution.py:366
  90.2 1.6 collective-permute-start.4
  91.8 23.1 %all-gather.2.cloned.1.call-done.act_ref = bf16[8,256,1024]{2,1,0:T(8,128)(2,1)} async-done(((bf16[1,256,1024]{2,1,0:T(8,128)(2,1)}), bf16[8,256,1024]{2,1,0:T(8,128)(2,1)}) %all-gather.2.cloned.1.call-update) | async-done | bytes 4194320 | tf_op jit(solution)/shard_map/all_gather | solution.py:421
  114.9 16.4 %weight_part.1 = f32[256,1792]{1,0:T(8,128)} custom-call(bf16[8,256,1024]{2,1,0:T(8,128)(2,1)} %all-gather.2.cloned.1.call-done.act_ref, bf16[64,8192]{1,0:T(8,128)(2,1)} %bitcast.99), custom_call_target="tpu_custom_call" | custom-call | flops 7247757312 | bytes 8388608 | tf_op jit(solution)/shard_map/weight_part/pallas_call | solution.py:249
  131.3 1.4 dynamic-slice_bitcast_fusion.1
  133.1 1.3 select_bitcast_fusion.5
  134.4 1.4 pad_maximum_fusion.1
  136.0 0.6 copy-done.2
  136.8 1.6 collective-permute-start.13
  138.5 1.0 copy-done.1
  139.4 1.1 fusion.2
  140.6 3.4 %collective-permute-start.9 = (bf16[256,1024]{1,0:T(8,128)(2,1)}, bf16[256,1024]{1,0:T(8,128)(2,1)}, u32[]{:S(2)}, u32[]{:S(2)}) collective-permute-start(bf16[256,1024]{1,0:T(8,128)(2,1)} %get-tuple-element.13), channel_id=1, source_target_pairs={{0,2},{1,3},{2,4},{3,5},{4,6},{5,7},{8,10},{9,11},{10,12},{11,13},... | collective-permute-start | bytes 1572872 | tf_op jit(solution)/shard_map/ppermute | solution.py:382
  144.0 1.3 collective-permute-start.10
  145.3 4.2 %collective-permute-done.13 = f32[8,8,1792]{2,1,0:T(8,128)S(1)} collective-permute-done((f32[8,8,1792]{2,1,0:T(8,128)S(1)}, f32[8,8,1792]{2,1,0:T(8,128)S(1)}, u32[]{:S(2)}, u32[]{:S(2)}) %collective-permute-start.13) | collective-permute-done | bytes 458784 | tf_op jit(solution)/shard_map/ppermute | solution.py:396
  149.5 0.8 bitcast_add_fusion.1
  150.3 4.9 %all-to-all-start = ((f32[8,8,1792]{2,1,0:T(8,128)}), f32[8,8,1792]{2,1,0:T(8,128)}, u32[]{:S(2)}, u32[]{:S(2)}) async-start(f32[8,8,1792]{2,1,0:T(8,128)} %bitcast_add_fusion.1), calls=%async_computation | async-start | bytes 917504 | tf_op jit(solution)/shard_map/all_to_all | solution.py:397
  155.8 2.3 copy.31
  158.1 2.8 %collective-permute-done.10.above_ref = bf16[256,1024]{1,0:T(8,128)(2,1)} collective-permute-done((bf16[256,1024]{1,0:T(8,128)(2,1)}, bf16[256,1024]{1,0:T(8,128)(2,1)}, u32[]{:S(2)}, u32[]{:S(2)}) %collective-permute-start.10) | collective-permute-done | bytes 524320 | tf_op jit(solution)/shard_map/ppermute | solution.py:383
  160.9 8.2 %input_part.3 = f32[256,1024]{1,0:T(8,128)} custom-call(s32[1]{0:T(128)S(6)} %sub.27.which_ref, bf16[256,1024]{1,0:T(8,128)(2,1)} %collective-permute-done.9.below_ref, bf16[256,2048]{1,0:T(8,128)(2,1)} %bitcast.95, bf16[256,1024]{1,0:T(8,128)(2,1)} %collective-permute-done.10.above_ref, bf16[3,9,256,256]{3,2,1,0:T(8,128)(2,1)} %bitcast.90), custom_call_target="tpu_custom_call" | custom-call | flops 3623878656 | bytes 8388608 | tf_op jit(solution)/shard_map/input_part/pallas_call | solution.py:296
  169.1 1.3 all-to-all-done
  170.4 0.5 collective-permute-start.14
  170.9 1.8 dynamic-slice_bitcast_fusion
  172.7 2.8 %copy.32 = bf16[9,64,3,256]{3,2,1,0:T(4,128)(2,1)S(1)} copy(bf16[9,64,3,256]{1,3,0,2:T(8,128)(2,1)} %dynamic-slice_bitcast_fusion) | data formatting | bytes 1769472 | tf_op jit(solution)/shard_map/transpose | solution.py:433
  175.5 1.1 copy.42
  176.6 0.3 copy-done.10
  177.0 0.8 collective-permute-start.11
  177.8 8.1 %input_part.2 = f32[256,1024]{1,0:T(8,128)} custom-call(s32[1]{0:T(128)} %bitcast.16.which_ref, bf16[256,1024]{1,0:T(8,128)(2,1)} %collective-permute-done.9.below_ref, bf16[256,2048]{1,0:T(8,128)(2,1)} %bitcast.96, bf16[256,1024]{1,0:T(8,128)(2,1)} %collective-permute-done.10.above_ref, bf16[3,9,256,256]{3,2,1,0:T(8,128)(2,1)} %bitcast.91), custom_call_target="tpu_custom_call" | custom-call | flops 3623878656 | bytes 8388608 | tf_op jit(solution)/shard_map/input_part/pallas_call | solution.py:296
  185.9 1.3 select_bitcast_fusion.7
  187.3 13.2 %collective-permute-done.11 = f32[256,1024]{1,0:T(8,128)S(1)} collective-permute-done((f32[256,1024]{1,0:T(8,128)S(1)}, f32[256,1024]{1,0:T(8,128)S(1)}, u32[]{:S(2)}, u32[]{:S(2)}) %collective-permute-start.11) | collective-permute-done | bytes 1048608 | tf_op jit(solution)/shard_map/ppermute | solution.py:428
  200.5 0.9 fusion
  201.4 16.7 %forward.1 = bf16[64,8192]{1,0:T(8,128)(2,1)} custom-call(bf16[2048,1024]{1,0:T(8,128)(2,1)} %bitcast.102, bf16[576,768]{1,0:T(8,128)(2,1)} %bitcast.100, f32[64,1]{1,0:T(8,128)} %copy.33.bias_ref), custom_call_target="tpu_custom_call" | custom-call | flops 7247757312 | bytes 6291456 | tf_op jit(solution)/shard_map/forward/pallas_call | solution.py:172
  218.3 1.4 pad_maximum_fusion
  219.7 3.3 %arrange.1 = f32[27,32,512]{2,1,0:T(8,128)} custom-call(f32[1]{0:T(128)} %copy.55.scale_ref, f32[8,32,1792]{2,1,0:T(8,128)} %bitcast.88), custom_call_target="tpu_custom_call" | custom-call | tf_op jit(solution)/shard_map/arrange/pallas_call | solution.py:336
  222.9 1.0 dynamic-slice_bitcast_fusion.6
  223.9 0.6 fusion.1
  (60 shorter events, 2.5 us)
Async XLA Ops:
  7.2 107.7 %all-gather.2.cloned.1.call-start = ((), (), s32[]{:S(2)}) async-start(), calls=%async_computation.1 | async-start | bytes 4718592 | tf_op jit(solution)/shard_map/all_gather | solution.py:421
  7.9 10.3 %copy-start.3 = (bf16[1,64,8192]{2,1,0:T(8,128)(2,1)S(1)}, bf16[1,64,8192]{2,1,0:T(8,128)(2,1)}, u32[]{:S(2)}) copy-start(bf16[1,64,8192]{2,1,0:T(8,128)(2,1)} %param.8) | copy-start | bytes 3145732
  12.0 11.8 %copy-start.9 = (f32[64]{0:T(128)S(1)}, f32[64]{0:T(128)}, u32[]{:S(2)}) copy-start(f32[64]{0:T(128)} %param.7) | copy-start | bytes 772
  15.2 10.0 %collective-permute-start = (bf16[27,8,256]{2,1,0:T(8,128)(2,1)S(1)}, bf16[27,8,256]{2,1,0:T(8,128)(2,1)S(1)}, u32[]{:S(2)}, u32[]{:S(2)}) collective-permute-start(bf16[27,8,256]{2,1,0:T(8,128)(2,1)S(1)} %reshape.51), channel_id=1, source_target_pairs={{0,1},{1,0},{2,3},{3,2},{4,5},{5,4},{6,7},{7,6},{8,9},{9,8},{10,11... | collective-permute-start | bytes 331784 | tf_op jit(solution)/shard_map/ppermute | solution.py:365
  19.0 17.4 %collective-permute-start.6 = (bf16[64,2048]{1,0:T(8,128)(2,1)S(1)}, bf16[64,2048]{1,0:T(8,128)(2,1)S(1)}, u32[]{:S(2)}, u32[]{:S(2)}) collective-permute-start(bf16[64,2048]{1,0:T(8,128)(2,1)S(1)} %get-tuple-element.16), channel_id=1, source_target_pairs={{0,6},{1,7},{2,0},{3,1},{4,2},{5,3},{6,4},{7,5},{8,14},{9,15},{10,... | collective-permute-start | bytes 786440 | tf_op jit(solution)/shard_map/ppermute | solution.py:379
  22.6 49.8 %collective-permute-start.7 = (bf16[64,2048]{1,0:T(8,128)(2,1)}, bf16[64,2048]{1,0:T(8,128)(2,1)S(1)}, u32[]{:S(2)}, u32[]{:S(2)}) collective-permute-start(bf16[64,2048]{1,0:T(8,128)(2,1)} %get-tuple-element.15), channel_id=1, source_target_pairs={{0,4},{1,5},{2,6},{3,7},{4,0},{5,1},{6,2},{7,3},{8,12},{9,13},{10,... | collective-permute-start | bytes 786440 | tf_op jit(solution)/shard_map/ppermute | solution.py:379
  22.6 49.8 %collective-permute-start.8 = (bf16[64,2048]{1,0:T(8,128)(2,1)S(1)}, bf16[64,2048]{1,0:T(8,128)(2,1)S(1)}, u32[]{:S(2)}, u32[]{:S(2)}) collective-permute-start(bf16[64,2048]{1,0:T(8,128)(2,1)S(1)} %get-tuple-element.14), channel_id=1, source_target_pairs={{0,2},{1,3},{2,4},{3,5},{4,6},{5,7},{6,0},{7,1},{8,10},{9,11},{10,... | collective-permute-start | bytes 786440 | tf_op jit(solution)/shard_map/ppermute | solution.py:379
  25.3 47.3 %collective-permute-start.1 = (bf16[2,27,8,256]{3,2,1,0:T(8,128)(2,1)S(1)}, bf16[2,27,8,256]{3,2,1,0:T(8,128)(2,1)S(1)}, u32[]{:S(2)}, u32[]{:S(2)}) collective-permute-start(bf16[2,27,8,256]{3,2,1,0:T(8,128)(2,1)S(1)} %pad_maximum_fusion.3), channel_id=1, source_target_pairs={{0,6},{1,7},{2,0},{3,1},{4,2},{5,3},{6,4},{7,5},{8,14},{9,15},{10,... | collective-permute-start | bytes 663560 | tf_op jit(solution)/shard_map/ppermute | solution.py:366
  28.2 61.8 %collective-permute-start.2 = (bf16[2,27,8,256]{3,2,1,0:T(8,128)(2,1)S(1)}, bf16[2,27,8,256]{3,2,1,0:T(8,128)(2,1)S(1)}, u32[]{:S(2)}, u32[]{:S(2)}) collective-permute-start(bf16[2,27,8,256]{3,2,1,0:T(8,128)(2,1)S(1)} %pad_maximum_fusion.3), channel_id=1, source_target_pairs={{0,4},{1,5},{2,6},{3,7},{4,0},{5,1},{6,2},{7,3},{8,12},{9,13},{10,... | collective-permute-start | bytes 663560 | tf_op jit(solution)/shard_map/ppermute | solution.py:366
  36.4 53.5 %collective-permute-start.3 = (bf16[2,27,8,256]{3,2,1,0:T(8,128)(2,1)S(1)}, bf16[2,27,8,256]{3,2,1,0:T(8,128)(2,1)S(1)}, u32[]{:S(2)}, u32[]{:S(2)}) collective-permute-start(bf16[2,27,8,256]{3,2,1,0:T(8,128)(2,1)S(1)} %pad_maximum_fusion.3), channel_id=1, source_target_pairs={{0,2},{1,3},{2,4},{3,5},{4,6},{5,7},{6,0},{7,1},{8,10},{9,11},{10,... | collective-permute-start | bytes 663560 | tf_op jit(solution)/shard_map/ppermute | solution.py:366
  72.4 17.6 %copy-start.5 = (bf16[64,2048]{1,0:T(8,128)(2,1)}, bf16[64,2048]{1,0:T(8,128)(2,1)S(1)}, u32[]{:S(2)}) copy-start(bf16[64,2048]{1,0:T(8,128)(2,1)S(1)} %collective-permute-done.8) | copy-start | bytes 786436
  72.5 17.5 %copy-start.7 = (bf16[7,64,2048]{2,1,0:T(8,128)(2,1)}, bf16[7,64,2048]{2,1,0:T(8,128)(2,1)S(1)}, u32[]{:S(2)}) copy-start(bf16[7,64,2048]{2,1,0:T(8,128)(2,1)S(1)} %bitcast_dynamic-update-slice_fusion.5) | copy-start | bytes 5505028
  90.2 42.9 %collective-permute-start.4 = (bf16[4,2,27,8,256]{4,3,2,1,0:T(8,128)(2,1)S(1)}, bf16[4,2,27,8,256]{4,3,2,1,0:T(8,128)(2,1)}, u32[]{:S(2)}, u32[]{:S(2)}) collective-permute-start(bf16[4,2,27,8,256]{4,3,2,1,0:T(8,128)(2,1)S(1)} %constant_dynamic-slice_fusion.1), channel_id=1, source_target_pairs={{0,16},{8,24},{16,0},{24,8},{1,17},{9,25},{17,1},{25,9},{2,18},{10... | collective-permute-start | bytes 2654216 | tf_op jit(solution)/shard_map/ppermute | solution.py:367
  131.3 1.8 copy-start.8
  132.7 3.3 %collective-permute-start.12 = (f32[8,2,8,1792]{3,2,1,0:T(8,128)S(1)}, f32[8,2,8,1792]{3,2,1,0:T(8,128)S(1)}, u32[]{:S(2)}, u32[]{:S(2)}) collective-permute-start(f32[8,2,8,1792]{3,2,1,0:T(8,128)S(1)} %dynamic-slice_bitcast_fusion.1), channel_id=1, source_target_pairs={{0,8},{8,0},{16,24},{24,16},{1,9},{9,1},{17,25},{25,17},{2,10},{10... | collective-permute-start | bytes 2752520 | tf_op jit(solution)/shard_map/ppermute | solution.py:395
  134.4 1.6 copy-start.6
  134.4 2.2 copy-start.2
  135.8 19.4 %collective-permute-start.5 = (bf16[2,4,2,27,8,256]{5,4,3,2,1,0:T(8,128)(2,1)}, bf16[2,4,2,27,8,256]{5,4,3,2,1,0:T(8,128)(2,1)S(1)}, u32[]{:S(2)}, u32[]{:S(2)}) collective-permute-start(bf16[2,4,2,27,8,256]{5,4,3,2,1,0:T(8,128)(2,1)} %pad_maximum_fusion.1), channel_id=1, source_target_pairs={{0,8},{8,0},{16,24},{24,16},{1,9},{9,1},{17,25},{25,17},{2,10},{10... | collective-permute-start | bytes 5308424 | tf_op jit(solution)/shard_map/ppermute | solution.py:368
  136.8 12.7 %collective-permute-start.13 = (f32[8,8,1792]{2,1,0:T(8,128)S(1)}, f32[8,8,1792]{2,1,0:T(8,128)S(1)}, u32[]{:S(2)}, u32[]{:S(2)}) collective-permute-start(f32[8,8,1792]{2,1,0:T(8,128)S(1)} %dynamic-slice_bitcast_fusion.2), channel_id=1, source_target_pairs={{0,16},{8,24},{16,0},{24,8},{1,17},{9,25},{17,1},{25,9},{2,18},{10... | collective-permute-start | bytes 1376264 | tf_op jit(solution)/shard_map/ppermute | solution.py:396
  138.5 1.0 copy-start.1
  140.6 17.5 %collective-permute-start.9 = (bf16[256,1024]{1,0:T(8,128)(2,1)}, bf16[256,1024]{1,0:T(8,128)(2,1)}, u32[]{:S(2)}, u32[]{:S(2)}) collective-permute-start(bf16[256,1024]{1,0:T(8,128)(2,1)} %get-tuple-element.13), channel_id=1, source_target_pairs={{0,2},{1,3},{2,4},{3,5},{4,6},{5,7},{8,10},{9,11},{10,12},{11,13},... | collective-permute-start | bytes 1572872 | tf_op jit(solution)/shard_map/ppermute | solution.py:382
  144.0 16.9 %collective-permute-start.10 = (bf16[256,1024]{1,0:T(8,128)(2,1)}, bf16[256,1024]{1,0:T(8,128)(2,1)}, u32[]{:S(2)}, u32[]{:S(2)}) collective-permute-start(bf16[256,1024]{1,0:T(8,128)(2,1)} %get-tuple-element.12), channel_id=1, source_target_pairs={{2,0},{3,1},{4,2},{5,3},{6,4},{7,5},{10,8},{11,9},{12,10},{13,11},... | collective-permute-start | bytes 1572872 | tf_op jit(solution)/shard_map/ppermute | solution.py:383
  150.3 20.1 %all-to-all-start = ((f32[8,8,1792]{2,1,0:T(8,128)}), f32[8,8,1792]{2,1,0:T(8,128)}, u32[]{:S(2)}, u32[]{:S(2)}) async-start(f32[8,8,1792]{2,1,0:T(8,128)} %bitcast_add_fusion.1), calls=%async_computation | async-start | bytes 917504 | tf_op jit(solution)/shard_map/all_to_all | solution.py:397
  160.9 10.0 %copy-start = (bf16[27,4,2,2,2,8,256]{6,5,4,3,2,1,0:T(8,128)(2,1)S(1)}, bf16[27,4,2,2,2,8,256]{6,5,4,3,2,1,0:T(8,128)(2,1)}, u32[]{:S(2)}) copy-start(bf16[27,4,2,2,2,8,256]{6,5,4,3,2,1,0:T(8,128)(2,1)} %copy.31) | copy-start | bytes 10616836
  170.4 15.4 %collective-permute-start.14 = (f32[8,8,1792]{2,1,0:T(8,128)}, f32[8,8,1792]{2,1,0:T(8,128)}, u32[]{:S(2)}, u32[]{:S(2)}) collective-permute-start(f32[8,8,1792]{2,1,0:T(8,128)} %all-to-all-done), channel_id=1, source_target_pairs={{0,16},{8,24},{16,0},{24,8},{1,17},{9,25},{17,1},{25,9},{2,18},{10... | collective-permute-start | bytes 1376264 | tf_op jit(solution)/shard_map/ppermute | solution.py:398
  175.5 1.5 copy-start.10
  177.0 23.5 %collective-permute-start.11 = (f32[256,1024]{1,0:T(8,128)S(1)}, f32[256,1024]{1,0:T(8,128)S(1)}, u32[]{:S(2)}, u32[]{:S(2)}) collective-permute-start(f32[256,1024]{1,0:T(8,128)S(1)} %copy-done.10), channel_id=1, source_target_pairs={{0,1},{1,0},{2,3},{3,2},{4,5},{5,4},{6,7},{7,6},{8,9},{9,8},{10,11... | collective-permute-start | bytes 3145736 | tf_op jit(solution)/shard_map/ppermute | solution.py:428
  185.9 14.6 %copy-start.4 = (f32[256,1024]{1,0:T(8,128)S(1)}, f32[256,1024]{1,0:T(8,128)}, u32[]{:S(2)}) copy-start(f32[256,1024]{1,0:T(8,128)} %input_part.2) | copy-start | bytes 3145732
  187.2 30.9 %collective-permute-start.15 = (f32[2,8,8,1792]{3,2,0,1:T(8,128)S(1)}, f32[2,8,8,1792]{3,2,0,1:T(8,128)S(1)}, u32[]{:S(2)}, u32[]{:S(2)}) collective-permute-start(f32[2,8,8,1792]{3,2,0,1:T(8,128)S(1)} %pad_maximum_fusion.2), channel_id=1, source_target_pairs={{0,8},{8,0},{16,24},{24,16},{1,9},{9,1},{17,25},{25,17},{2,10},{10... | collective-permute-start | bytes 2752520 | tf_op jit(solution)/shard_map/ppermute | solution.py:399
Sparse Core Ops, SparseCore 0:
  10.1 104.7 all-gather.1

commit v2 on v0

--- a/solution.py
+++ b/solution.py
@@ -1,6 +1,10 @@
+import functools
+
 import jax
 import jax.numpy as jnp
 from jax import lax
+from jax.experimental import pallas as pl
+from jax.experimental.pallas import tpu as pltpu
 from jax.sharding import PartitionSpec as P
 
 SIDE = 32
@@ -70,7 +74,7 @@
     return (input_grad, weight_part.reshape(27, patches.shape[0] // 27, every_grad.shape[0]))
 
 
-def per_device(activations, weights, conv_bias, grad_out, loss_scale):
+def shard_general(activations, weights, conv_bias, grad_out, loss_scale):
     cell_count = grad_out.shape[2]
     channel_share = weights.shape[1]
     ahead = tap_valid(cell_count, SIDE, 1)
@@ -95,9 +99,468 @@
     return (conv_out, grad_input, weight_total / loss_scale[0], bias_total / loss_scale[0])
 
 
+VMEM_BYTES = 56 * 1024 * 1024
+PLANE = SIDE * SIDE
+TAPS = 27
+
+
+def in_plane():
+    cell = lax.broadcasted_iota(jnp.int32, (1, PLANE), 1)
+    return cell // SIDE, cell % SIDE
+
+
+def shifted(value, offset):
+    return pltpu.roll(value, (-offset) % PLANE, 1)
+
+
+def inside(coordinate, step):
+    moved = coordinate + step
+    return (moved >= 0) & (moved < SIDE)
+
+
+def gather_shifts(terms_ref, rows, sign):
+    line, position = in_plane()
+    total = None
+    for c in range(3):
+        column = None
+        for b in range(3):
+            start = (3 * b + c) * rows
+            term = terms_ref[start : start + rows, :]
+            if b != 1:
+                term = jnp.where(
+                    inside(line, sign * (b - 1)), shifted(term, sign * SIDE * (b - 1)), 0.0
+                )
+            column = term if column is None else column + term
+        if c != 1:
+            column = jnp.where(
+                inside(position, sign * (c - 1)), shifted(column, sign * (c - 1)), 0.0
+            )
+        total = column if total is None else total + column
+    return total
+
+
+def in_turn(multiply, finish, terms_refs, count):
+    for step in range(count + 1):
+        if step < count:
+            multiply(step, terms_refs[step % 2])
+        if step:
+            finish(step - 1, terms_refs[(step - 1) % 2])
+
+
+def forward_kernel(place_ref, *refs):
+    block_refs = refs[:8]
+    kernel_ref, bias_ref, out_ref, act_ref, even_ref, odd_ref, sems = refs[8:]
+    channels = act_ref.shape[0] // 8
+    filters = bias_ref.shape[0]
+    copies = []
+    for index, block_ref in enumerate(block_refs):
+        start = pl.multiple_of(place_ref[index] * channels, channels)
+        copies.append(
+            pltpu.make_async_copy(block_ref, act_ref.at[pl.ds(start, channels), :], sems.at[index])
+        )
+    for copy in copies:
+        copy.start()
+    for copy in copies:
+        copy.wait()
+
+    def multiply(plane, into_ref):
+        first, last = max(plane - 1, 0), min(plane + 2, 8)
+        lanes = (first - plane + 1) * channels
+        into_ref[...] = jnp.dot(
+            kernel_ref[:, lanes : lanes + (last - first) * channels],
+            act_ref[first * channels : last * channels, :],
+            preferred_element_type=jnp.float32,
+        )
+
+    def finish(plane, from_ref):
+        total = gather_shifts(from_ref, filters, 1) + bias_ref[...]
+        out_ref[:, plane * PLANE : (plane + 1) * PLANE] = total.astype(out_ref.dtype)
+
+    in_turn(multiply, finish, (even_ref, odd_ref), 8)
+
+
+def forward(place, blocks, kernel, bias):
+    channels, cells = blocks[0].shape
+    filters = bias.shape[0]
+    vmem = pl.BlockSpec(memory_space=pltpu.VMEM)
+    return pl.pallas_call(
+        forward_kernel,
+        in_specs=[pl.BlockSpec(memory_space=pltpu.SMEM)]
+        + [pl.BlockSpec(memory_space=pl.ANY)] * 8
+        + [vmem, vmem],
+        out_specs=vmem,
+        out_shape=jax.ShapeDtypeStruct((filters, 8 * cells), jnp.bfloat16),
+        scratch_shapes=[
+            pltpu.VMEM((8 * channels, cells), jnp.bfloat16),
+            pltpu.VMEM((9 * filters, cells), jnp.float32),
+            pltpu.VMEM((9 * filters, cells), jnp.float32),
+            pltpu.SemaphoreType.DMA((8,)),
+        ],
+        compiler_params=pltpu.CompilerParams(vmem_limit_bytes=VMEM_BYTES),
+        cost_estimate=pl.CostEstimate(
+            flops=2 * TAPS * channels * filters * 8 * cells,
+            bytes_accessed=6 * 1024 * 1024,
+            transcendentals=0,
+        ),
+        name="forward",
+    )(place, *blocks, kernel, bias[:, None])
+
+
+def weight_kernel(first, last, place_ref, grad_ref, near_ref, far_ref, *refs):
+    before_ref = None if first else refs[0]
+    *out_refs, moved_ref, act_ref, total_ref = refs if first else refs[1:]
+    filters = grad_ref.shape[0]
+    group = 9 * filters
+    pair, x = place_ref[0], place_ref[1]
+    line, position = in_plane()
+
+    def lanes_of(index):
+        return pl.ds(pl.multiple_of(index * PLANE, PLANE), PLANE)
+
+    act_ref[:, lanes_of(x)] = near_ref[...]
+    act_ref[:, lanes_of(1 - x)] = far_ref[...]
+    bias = None
+    for place in range(4):
+        plane = 2 * pair - 1 + place
+        lanes = slice(place * PLANE, (place + 1) * PLANE)
+        held = jnp.clip(plane, 0, 7)
+        block = grad_ref[:, lanes_of(held)].astype(jnp.float32)
+        if place in (0, 3):
+            block = jnp.where(held == plane, block, 0.0)
+        else:
+            share = jnp.sum(block, axis=1, keepdims=True)
+            bias = share if bias is None else bias + share
+        for c in range(3):
+            column = block
+            if c != 1:
+                column = jnp.where(
+                    inside(position, -(c - 1)), shifted(block, -(c - 1)), 0.0
+                )
+            for b in range(3):
+                term = column
+                if b != 1:
+                    term = jnp.where(
+                        inside(line, -(b - 1)), shifted(column, -SIDE * (b - 1)), 0.0
+                    )
+                start = (3 * b + c) * filters
+                moved_ref[start : start + filters, lanes] = term.astype(moved_ref.dtype)
+    for a in range(3):
+        rows = slice(a * group, (a + 1) * group)
+        total = lax.dot_general(
+            moved_ref[:, (2 - a) * PLANE : (4 - a) * PLANE],
+            act_ref[...],
+            (((1,), (1,)), ((), ())),
+            preferred_element_type=jnp.float32,
+        )
+        total_ref[rows, :] = total if first else before_ref[rows, :] + total
+    bias = jnp.broadcast_to(bias, (filters, total_ref.shape[1]))
+    total_ref[3 * group :, :] = bias if first else before_ref[3 * group :, :] + bias
+    if last:
+        turned = total_ref[...].T
+        halves = turned.reshape(8, 2, turned.shape[0] // 16, turned.shape[1])
+        own, other = halves[:, 0], halves[:, 1]
+        core = place_ref[2]
+        out_refs[0][...] = jnp.where(core == 0, own, other)
+        out_refs[1][...] = jnp.where(core == 0, other, own)
+    else:
+        out_refs[0][...] = total_ref[...]
+
+
+def weight_part(place, grads, near, far, before, last):
+    channels, cells = near.shape
+    filters = grads.shape[0]
+    width = (TAPS + 1) * filters
+    vmem = pl.BlockSpec(memory_space=pltpu.VMEM)
+    first = before is None
+    operands = [place, grads, near, far] + ([] if first else [before])
+    return pl.pallas_call(
+        functools.partial(weight_kernel, first, last),
+        in_specs=[pl.BlockSpec(memory_space=pltpu.SMEM)] + [vmem] * (len(operands) - 1),
+        out_specs=[vmem, vmem] if last else vmem,
+        out_shape=[jax.ShapeDtypeStruct((8, channels // 16, width), jnp.float32)] * 2
+        if last
+        else jax.ShapeDtypeStruct((width, channels), jnp.float32),
+        scratch_shapes=[
+            pltpu.VMEM((9 * filters, 4 * cells), jnp.bfloat16),
+            pltpu.VMEM((channels, 2 * cells), jnp.bfloat16),
+            pltpu.VMEM((width, channels), jnp.float32),
+        ],
+        compiler_params=pltpu.CompilerParams(vmem_limit_bytes=VMEM_BYTES),
+        cost_estimate=pl.CostEstimate(
+            flops=2 * TAPS * channels * filters * 2 * cells,
+            bytes_accessed=5 * 1024 * 1024,
+            transcendentals=0,
+        ),
+        name="weight_part",
+    )(*operands)
+
+
+def input_kernel(
+    which_ref, below_ref, middle_ref, above_ref, weights_ref, out_ref,
+    planes_ref, kernel_ref, even_ref, odd_ref, sems,
+):
+    filters = below_ref.shape[0]
+    parts, _, rows, _ = kernel_ref.shape
+    copies = []
+    for part in range(parts):
+        copies.append([])
+        for index in range(8):
+            quarter, x = index // 2, index % 2
+            to_ref = kernel_ref.at[part, pl.ds(7 * quarter, 7), pl.ds(32 * x, 32), :]
+            copies[-1].append(
+                pltpu.make_async_copy(
+                    weights_ref.at[quarter % 2, quarter // 2, part, x], to_ref, sems.at[part, index]
+                )
+            )
+            copies[-1][-1].start()
+    planes_ref[:filters, :] = below_ref[...]
+    planes_ref[filters : 2 * filters, :] = middle_ref[:, :PLANE]
+    planes_ref[2 * filters : 3 * filters, :] = middle_ref[:, PLANE:]
+    planes_ref[3 * filters :, :] = above_ref[...]
+    start = pl.multiple_of(which_ref[0] * filters, filters)
+
+    def multiply(part, into_ref):
+        for copy in copies[part]:
+            copy.wait()
+        last = jnp.concatenate([kernel_ref[part, 18:21], kernel_ref[part, 22:28]])
+        groups = [last, kernel_ref[part, 9:18], kernel_ref[part, :9]]
+        kernel = jnp.concatenate(
+            [group.reshape(9 * rows, filters) for group in groups], axis=1
+        )
+        into_ref[...] = jnp.dot(
+            kernel, planes_ref[pl.ds(start, 3 * filters), :], preferred_element_type=jnp.float32
+        )
+
+    def finish(part, from_ref):
+        out_ref[part * rows : (part + 1) * rows, :] = gather_shifts(from_ref, rows, -1)
+
+    in_turn(multiply, finish, (even_ref, odd_ref), parts)
+
+
+def input_part(which, below, middle, above, kernel, rows=64):
+    filters, cells = below.shape
+    channels = 4 * rows
+    vmem = pl.BlockSpec(memory_space=pltpu.VMEM)
+    return pl.pallas_call(
+        input_kernel,
+        in_specs=[
+            pl.BlockSpec(memory_space=pltpu.SMEM),
+            vmem,
+            vmem,
+            vmem,
+            pl.BlockSpec(memory_space=pl.ANY),
+        ],
+        out_specs=vmem,
+        out_shape=jax.ShapeDtypeStruct((channels, cells), jnp.float32),
+        scratch_shapes=[
+            pltpu.VMEM((4 * filters, cells), jnp.bfloat16),
+            pltpu.VMEM((channels // rows, 28, rows, filters), jnp.bfloat16),
+            pltpu.VMEM((9 * rows, cells), jnp.float32),
+            pltpu.VMEM((9 * rows, cells), jnp.float32),
+            pltpu.SemaphoreType.DMA((channels // rows, 8)),
+        ],
+        compiler_params=pltpu.CompilerParams(vmem_limit_bytes=VMEM_BYTES),
+        cost_estimate=pl.CostEstimate(
+            flops=2 * TAPS * channels * filters * cells,
+            bytes_accessed=8 * 1024 * 1024,
+            transcendentals=0,
+        ),
+        name="input_part",
+    )(which, below, middle, above, kernel)
+
+
+def pick_kernel(place_ref, weights_ref, own_ref, other_ref):
+    count, rows, width = own_ref.shape
+    x = place_ref[1]
+    taps = weights_ref[pl.ds(place_ref[0], count)].reshape(count * rows, 2 * width)
+    taps = taps.astype(jnp.float32)
+    left = lax.broadcasted_iota(jnp.int32, (1, 128), 1) < 64
+    for block in range(width // 128):
+        first = taps[:, 256 * block : 256 * block + 128]
+        second = taps[:, 256 * block + 128 : 256 * block + 256]
+        even = jnp.where(left, first, pltpu.roll(second, 64, 1))
+        odd = jnp.where(left, pltpu.roll(first, 64, 1), second)
+        lanes = slice(128 * block, 128 * block + 128)
+        own, other = jnp.where(x == 0, even, odd), jnp.where(x == 0, odd, even)
+        own_ref[:, :, lanes] = own.astype(own_ref.dtype).reshape(count, rows, 128)
+        other_ref[:, :, lanes] = other.astype(own_ref.dtype).reshape(count, rows, 128)
+
+
+def pick(place, weights, count):
+    _, rows, filters = weights.shape
+    vmem = pl.BlockSpec(memory_space=pltpu.VMEM)
+    return pl.pallas_call(
+        pick_kernel,
+        in_specs=[pl.BlockSpec(memory_space=pltpu.SMEM), vmem],
+        out_specs=[vmem, vmem],
+        out_shape=[jax.ShapeDtypeStruct((count, rows, filters // 2), weights.dtype)] * 2,
+        compiler_params=pltpu.CompilerParams(vmem_limit_bytes=VMEM_BYTES),
+        name="pick",
+    )(place, weights)
+
+
+def arrange_kernel(scale_ref, core_ref, own_ref, other_ref, out_ref):
+    _, sources, rows, width = own_ref.shape
+    filters = width // (TAPS + 1)
+    scale = scale_ref[0]
+    for near, ref in ((True, own_ref), (False, other_ref)):
+        core = core_ref[0] if near else 1 - core_ref[0]
+        for y in range(2):
+            at = pl.ds(pl.multiple_of((2 * core + y) * rows, rows), rows)
+            for source in range(sources):
+                block = ref[y, source] / scale
+                for tap in range(TAPS):
+                    out_ref[tap, at, source * filters : (source + 1) * filters] = block[
+                        :, tap * filters : (tap + 1) * filters
+                    ]
+
+
+def arrange(scale, core, own, other):
+    _, sources, rows, width = own.shape
+    filters = width // (TAPS + 1)
+    vmem, smem = pl.BlockSpec(memory_space=pltpu.VMEM), pl.BlockSpec(memory_space=pltpu.SMEM)
+    return pl.pallas_call(
+        arrange_kernel,
+        in_specs=[smem, smem, vmem, vmem],
+        out_specs=vmem,
+        out_shape=jax.ShapeDtypeStruct((TAPS, 4 * rows, sources * filters), jnp.float32),
+        compiler_params=pltpu.CompilerParams(vmem_limit_bytes=VMEM_BYTES),
+        name="arrange",
+    )(scale, core, own, other)
+
+
+def after(value, *earlier):
+    return lax.optimization_barrier((value,) + earlier)[0]
+
+
+def in_order(own, other, bit):
+    return jnp.stack([jnp.where(bit == 0, own, other), jnp.where(bit == 0, other, own)])
+
+
+def by_source(received, own_index):
+    count = len(received)
+    falling = jnp.stack(received[::-1] + received[::-1][:-1])
+    return lax.dynamic_slice_in_dim(falling, count - 1 - own_index, count, 0)
+
+
+def half(array, axis, index):
+    return lax.dynamic_index_in_dim(array, index, axis, False)
+
+
+def placement():
+    grp, sp = lax.axis_index("grp"), lax.axis_index("sp")
+    return {
+        "z": sp // 2,
+        "x": sp % 2,
+        "y": grp // 2,
+        "core": grp % 2,
+        "swap_x": [(s, s ^ 1) for s in range(8)],
+        "swap_core": [(g, g ^ 1) for g in range(4)],
+        "swap_y": [(g, g ^ 2) for g in range(4)],
+        "pair_z": [(s, s ^ 2) for s in range(8)],
+        "cross_z": [(2, 4), (3, 5), (4, 2), (5, 3)],
+        "out_z": [(2, 0), (3, 1), (4, 6), (5, 7)],
+        "turn_z1": [(s, (s + 2) % 8) for s in range(8)],
+        "turn_z2": [(s, (s + 4) % 8) for s in range(8)],
+        "turn_z3": [(s, (s + 6) % 8) for s in range(8)],
+        "up_z": [(s, s + 2) for s in range(6)],
+        "down_z": [(s + 2, s) for s in range(6)],
+    }
+
+
+def per_device(activations, weights, conv_bias, grad_out, loss_scale):
+    at = placement()
+    z, x, y, core = at["z"], at["x"], at["y"], at["core"]
+    together = lax.optimization_barrier
+    grads = grad_out[0]
+    inner = (z == 1) | (z == 2)
+    sources = [z, z ^ 1, jnp.where(z < 2, 2, 1), jnp.where(z < 2, 3, 0)]
+
+    def along(value, axis, steps):
+        return lax.ppermute(value, axis, at[steps])
+
+    def add_pair(index, part):
+        place = jnp.stack([sources[index], x, core]).astype(jnp.int32)
+        return weight_part(place, grads, near[index], far[index], part, index == 3)
+
+    def planes_for(k):
+        return lax.dynamic_slice_in_dim(grads, ((z + k) % 4) * 2 * PLANE, 2 * PLANE, 1)
+
+    own = activations[0]
+    second = along(own, "sp", "pair_z")
+    third = along(own, "sp", "cross_z")
+    own_far = along(own, "sp", "swap_x")
+    first_tap = jnp.minimum(7 * (2 * y + core), TAPS - 7)
+    keep, give = pick(jnp.stack([first_tap, x]).astype(jnp.int32), weights, 7)
+    given = along(give, "sp", "swap_x")
+    second, third, own_far, given = together((second, third, own_far, given))
+
+    near, far = [own], [own_far]
+    fourth = along(second, "sp", "cross_z")
+    third_out = along(third, "sp", "out_z")
+    near.append(second)
+    far.append(along(second, "sp", "swap_x"))
+    kernel = in_order(keep, given, x)
+    ring = [kernel] + [along(kernel, "sp", f"turn_z{k}") for k in (1, 2, 3)]
+    part = add_pair(0, None)
+    fourth, third_out, far[1], part = together((fourth, third_out, far[1], part))
+
+    near.append(jnp.where(inner, third, third_out))
+    far.append(along(near[2], "sp", "swap_x"))
+    fourth_out = along(fourth, "sp", "out_z")
+    part = add_pair(1, part)
+    fourth_out, far[2], part, *ring = together((fourth_out, far[2], part, *ring))
+
+    near.append(jnp.where(inner, fourth, fourth_out))
+    far.append(along(near[3], "sp", "swap_x"))
+    grads = after(grads, fourth_out)
+    blocks = [planes_for(0)] + [along(planes_for(k), "sp", f"turn_z{k}") for k in (1, 2, 3)]
+    kernel = by_source(ring, z)
+    arrived = along(kernel, "grp", "swap_y")
+    rows, give = add_pair(3, add_pair(2, part))
+    rows, give, arrived, *blocks = together((rows, give, arrived, *blocks))
+
+    middle = by_source(blocks, z).reshape(256, 2 * PLANE)
+    below = along(middle[:, PLANE:], "sp", "up_z")
+    above = along(middle[:, :PLANE], "sp", "down_z")
+    given = along(give, "grp", "swap_core")
+    kernel = in_order(kernel, arrived, y)
+    kernel = in_order(kernel, along(kernel, "grp", "swap_core"), core)
+    own_filters = lax.dynamic_slice_in_dim(kernel, z * 64, 64, 6)
+    own_filters = own_filters.transpose(1, 0, 4, 6, 2, 3, 5).reshape(28, 64, 256)
+    own_filters = jnp.concatenate([own_filters[:21], own_filters[22:]])
+    own_filters = own_filters.reshape(3, 9 * 64, 256).transpose(1, 0, 2).reshape(9 * 64, 3 * 256)
+    width = rows.shape[2]
+    rows = (rows + given).reshape(8, 2, 8, width)
+    below, above, rows, kernel, own_filters = together((below, above, rows, kernel, own_filters))
+
+    arrived = along(half(rows, 1, 1 - y), "grp", "swap_y")
+    which = x.astype(jnp.int32)[None]
+    other_plane = input_part(1 - which, below, middle, above, kernel)
+    arrived, other_plane = together((arrived, other_plane))
+
+    other_plane = along(other_plane, "sp", "swap_x")
+    rows = lax.all_to_all(half(rows, 1, y) + arrived, "sp", 0, 0)
+    place = jnp.stack([2 * s + x for s in sources] + [2 * s + 1 - x for s in sources])
+    conv_out = forward(place.astype(jnp.int32), near + far, own_filters, conv_bias)
+    own_plane = input_part(which, below, middle, above, kernel)
+    arrived = along(rows, "grp", "swap_y")
+    rows, arrived, other_plane, own_plane, conv_out = together(
+        (rows, arrived, other_plane, own_plane, conv_out)
+    )
+
+    rows = in_order(rows, arrived, y)
+    other_rows = along(rows, "grp", "swap_core")
+    grad_weight = arrange(loss_scale, core.astype(jnp.int32)[None], rows, other_rows)
+    bias_sum = half(rows[0], 0, lax.axis_index("sp"))[0, TAPS * 64 :]
+    grad_input = (own_plane + other_plane).astype(jnp.bfloat16)
+    return (conv_out[None], grad_input[None], grad_weight, bias_sum / loss_scale[0])
+
+
 def solution(mesh):
+    measured = mesh.shape["grp"] == 4 and mesh.shape["sp"] == 8
     return jax.shard_map(
-        per_device,
+        per_device if measured else shard_general,
         mesh=mesh,
         in_specs=(P("grp", None, "sp"), P(None, "sp", None), P("sp"), P("grp", "sp", None), P()),
         out_specs=(P("grp", "sp", None), P("grp", None, "sp"), P(None, "sp", None), P("sp")),

time: 524 us -> 175 us (0.33)
  waiting for transfers between devices: 298 us -> 47.5 us
  other arithmetic: 96.3 us -> 13.7 us
  Pallas kernels: 0 us -> 59.6 us
  matrix products: 45.5 us -> 0 us
  local copies, waits for them, and re-layouts: 50.6 us -> 11.6 us
  starting transfers between devices: 11.3 us -> 40.1 us
  between operations: 14.6 us -> 1.82 us
  blocking collectives: 6.58 us -> 0 us
    unnamed x4 -> x0, waiting for transfers between devices: 181 us -> none
    all_gather x1 -> x0, waiting for transfers between devices: 87.1 us -> none  [per_device(): every_grad = lax.all_gather(grad_out, 'sp', axis=1, tiled=True)[0]]
    unnamed x28 -> x0, other arithmetic: 75.2 us -> none
    pallas_call x0 -> x9, Pallas kernels: none -> 59.6 us  [the longest x4 24.4 us: weight_part(): pl.pallas_call(functools.partial(weight_kernel, first, last), in_specs=[p...]
    dot_general x3 -> x0, matrix products: 45.5 us -> none  [the longest x1 16.1 us: local_backward(): jnp.einsum('kcf,fp->kcp', weights, every_grad, preferred_element_type=jnp...]
    ppermute x0 -> x25, waiting for transfers between devices: none -> 39.8 us  [along(): return lax.ppermute(value, axis, at[steps])]
    ppermute x0 -> x25, starting transfers between devices: none -> 36.5 us  [along(): return lax.ppermute(value, axis, at[steps])]
    unnamed x16 -> x44, local copies, waits for them, and re-layouts: 34.8 us -> 3.05 us
  transfers between devices with their start and end apart: 5 -> 26, of which waited for: 4 -> 9; matrix products, arithmetic and copies ran while one was open for 31% -> 12% of each run, Pallas kernels for 0% -> 32%
where the time goes in v2:
time: 175 us; the launch traced here: 174 us
  Pallas kernels  59.6 us (34%)
  waiting for transfers between devices  47.5 us (27%)
  starting transfers between devices  40.1 us (23%)
  other arithmetic  13.7 us (8%)
  local copies, waits for them, and re-layouts  11.6 us (7%)
  between operations  1.82 us (1%)
    ppermute x25, waiting for transfers between devices, along(): return lax.ppermute(value, axis, at[steps])  39.8 us
    ppermute x25, starting transfers between devices, along(): return lax.ppermute(value, axis, at[steps])  36.5 us
    pallas_call x4, Pallas kernels, weight_part(): pl.pallas_call(functools.partial(weight_kernel, first, last), in_specs=[p...  24.4 us
    pallas_call x2, Pallas kernels, input_part(): pl.pallas_call(input_kernel, in_specs=[pl.BlockSpec(memory_space=pltpu.SM...  18 us
    pallas_call x1, Pallas kernels, forward(): pl.pallas_call(forward_kernel, in_specs=[pl.BlockSpec(memory_space=pltpu....  11.9 us
    all_to_all x1, waiting for transfers between devices, per_device(): rows = lax.all_to_all(half(rows, 1, y) + arrived, 'sp', 0, 0)  7.75 us
    another operation x7, other arithmetic, in_order(): jnp.stack([jnp.where(bit == 0, own, other), jnp.where(bit == 0, other, ow...  4.36 us
    all_to_all x1, starting transfers between devices, per_device(): rows = lax.all_to_all(half(rows, 1, y) + arrived, 'sp', 0, 0)  3.53 us
  transfers between devices with their start and end apart: 26, of which 9 were waited for; matrix products, arithmetic and copies ran while one was open for 12% of the time, Pallas kernels for 32%

profile of v2, /device:TPU:0, one launch (start us, length us, event | category | flops | bytes accessed | tf_op | source)
XLA Modules:
  0.0 174.3 jit_solution(14179718761010438745)
XLA Ops:
  0.6 3.1 %collective-permute-start = (bf16[256,1024]{1,0:T(8,128)(2,1)}, bf16[256,1024]{1,0:T(8,128)(2,1)S(1)}, u32[]{:S(2)}, u32[]{:S(2)}) collective-permute-start(bf16[256,1024]{1,0:T(8,128)(2,1)} %bitcast.92), channel_id=1, source_target_pairs={{0,2},{1,3},{2,0},{3,1},{4,6},{5,7},{6,4},{7,5},{8,10},{9,11},{10,... | collective-permute-start | bytes 1572872 | tf_op jit(solution)/shard_map/ppermute | solution.py:480
  3.7 0.7 collective-permute-start.1
  4.4 1.6 collective-permute-start.2
  6.6 2.0 %pick.1 = (bf16[7,32,256]{2,1,0:T(8,128)(2,1)}, bf16[7,32,256]{2,1,0:T(8,128)(2,1)}) custom-call(s32[2]{0:T(128)} %pad_add_fusion.place_ref, bf16[27,32,512]{2,1,0:T(8,128)(2,1)} %weights_ref.1), custom_call_target="tpu_custom_call" | custom-call | tf_op jit(solution)/shard_map/pick/pallas_call | solution.py:392
  9.1 11.4 %collective-permute-done.3 = bf16[7,32,256]{2,1,0:T(8,128)(2,1)S(1)} collective-permute-done((bf16[7,32,256]{2,1,0:T(8,128)(2,1)}, bf16[7,32,256]{2,1,0:T(8,128)(2,1)S(1)}, u32[]{:S(2)}, u32[]{:S(2)}) %collective-permute-start.3) | collective-permute-done | bytes 114720 | tf_op jit(solution)/shard_map/ppermute | solution.py:480
  20.6 0.7 collective-permute-start.4
  21.3 1.3 collective-permute-start.5
  22.6 1.6 collective-permute-start.6
  24.7 5.5 %weight_part.4.refs_0_ = f32[1792,256]{1,0:T(8,128)} custom-call(s32[3]{0:T(128)} %add_add_fusion.1.place_ref, bf16[64,8192]{1,0:T(8,128)(2,1)} %bitcast.86, bf16[256,1024]{1,0:T(8,128)(2,1)} %bitcast.95, bf16[256,1024]{1,0:T(8,128)(2,1)} %copy-done.13), custom_call_target="tpu_custom_call" | custom-call | flops 1811939328 | bytes 5242880 | tf_op jit(solution)/shard_map/weight_part/pallas_call | solution.py:276
  30.2 8.3 %collective-permute-done.5 = bf16[256,1024]{1,0:T(8,128)(2,1)S(1)} collective-permute-done((bf16[256,1024]{1,0:T(8,128)(2,1)S(1)}, bf16[256,1024]{1,0:T(8,128)(2,1)S(1)}, u32[]{:S(2)}, u32[]{:S(2)}) %collective-permute-start.5) | collective-permute-done | bytes 524320 | tf_op jit(solution)/shard_map/ppermute | solution.py:480
  38.7 1.6 collective-permute-start.8
  40.2 1.3 collective-permute-start.7
  41.6 3.6 %collective-permute-start.10 = (bf16[2,7,32,256]{3,2,1,0:T(8,128)(2,1)S(1)}, bf16[2,7,32,256]{3,2,1,0:T(8,128)(2,1)S(1)}, u32[]{:S(2)}, u32[]{:S(2)}) collective-permute-start(bf16[2,7,32,256]{3,2,1,0:T(8,128)(2,1)S(1)} %pad_maximum_fusion.4), channel_id=1, source_target_pairs={{0,4},{1,5},{2,6},{3,7},{4,0},{5,1},{6,2},{7,3},{8,12},{9,13},{10,... | collective-permute-start | bytes 688136 | tf_op jit(solution)/shard_map/ppermute | solution.py:480
  45.2 1.5 collective-permute-start.11
  47.8 6.2 %weight_part.5.refs_0_ = f32[1792,256]{1,0:T(8,128)} custom-call(s32[3]{0:T(128)} %add_add_fusion.2.place_ref, bf16[64,8192]{1,0:T(8,128)(2,1)} %bitcast.87, bf16[256,1024]{1,0:T(8,128)(2,1)} %copy-done.12, bf16[256,1024]{1,0:T(8,128)(2,1)} %collective-permute-done.6.far_ref.refs_5_, f32[1792,256]{1,0:T(8,128)} %weight_part.4.refs_0_), custom_call_target="tpu_custom_call" | custom-call | flops 1811939328 | bytes 5242880 | tf_op jit(solution)/shard_map/weight_part/pallas_call | solution.py:276
  54.0 5.4 %collective-permute-done.10 = bf16[2,7,32,256]{3,2,1,0:T(8,128)(2,1)S(1)} collective-permute-done((bf16[2,7,32,256]{3,2,1,0:T(8,128)(2,1)S(1)}, bf16[2,7,32,256]{3,2,1,0:T(8,128)(2,1)S(1)}, u32[]{:S(2)}, u32[]{:S(2)}) %collective-permute-start.10) | collective-permute-done | bytes 229408 | tf_op jit(solution)/shard_map/ppermute | solution.py:480
  59.4 8.7 %collective-permute-done.11 = bf16[2,7,32,256]{3,2,1,0:T(8,128)(2,1)S(1)} collective-permute-done((bf16[2,7,32,256]{3,2,1,0:T(8,128)(2,1)S(1)}, bf16[2,7,32,256]{3,2,1,0:T(8,128)(2,1)S(1)}, u32[]{:S(2)}, u32[]{:S(2)}) %collective-permute-start.11) | collective-permute-done | bytes 229408 | tf_op jit(solution)/shard_map/ppermute | solution.py:480
  68.9 1.5 collective-permute-start.13
  71.9 2.6 %collective-permute-start.15 = (bf16[64,2048]{1,0:T(8,128)(2,1)S(1)}, bf16[64,2048]{1,0:T(8,128)(2,1)S(1)}, u32[]{:S(2)}, u32[]{:S(2)}) collective-permute-start(bf16[64,2048]{1,0:T(8,128)(2,1)S(1)} %get-tuple-element.89), channel_id=1, source_target_pairs={{0,4},{1,5},{2,6},{3,7},{4,0},{5,1},{6,2},{7,3},{8,12},{9,13},{10,... | collective-permute-start | bytes 786440 | tf_op jit(solution)/shard_map/ppermute | solution.py:480
  74.5 1.2 collective-permute-start.16
  75.7 6.1 %weight_part.6.refs_0_ = f32[1792,256]{1,0:T(8,128)} custom-call(s32[3]{0:T(128)} %get-tuple-element.97.place_ref, bf16[64,8192]{1,0:T(8,128)(2,1)} %bitcast.88, bf16[256,1024]{1,0:T(8,128)(2,1)} %copy-done.7, bf16[256,1024]{1,0:T(8,128)(2,1)} %copy-done.14, f32[1792,256]{1,0:T(8,128)} %weight_part.5.refs_0_), custom_call_target="tpu_custom_call" | custom-call | flops 1811939328 | bytes 5242880 | tf_op jit(solution)/shard_map/weight_part/pallas_call | solution.py:276
  82.2 0.8 copy-done.15
  83.0 6.6 %weight_part.7 = (f32[8,16,1792]{2,1,0:T(8,128)}, f32[8,16,1792]{2,1,0:T(8,128)}) custom-call(s32[3]{0:T(128)} %get-tuple-element.96.place_ref, bf16[64,8192]{1,0:T(8,128)(2,1)} %bitcast.89, bf16[256,1024]{1,0:T(8,128)(2,1)} %copy-done.8, bf16[256,1024]{1,0:T(8,128)(2,1)} %copy-done.15, f32[1792,256]{1,0:T(8,128)} %weight_part.6.refs_0_), custom_call_target="tpu_custom_call" | custom-call | flops 1811939328 | bytes 5242880 | tf_op jit(solution)/shard_map/weight_part/pallas_call | solution.py:276
  89.6 1.3 collective-permute-done.15
  91.3 0.9 copy-done.11
  92.5 0.9 fusion.4
  93.4 7.9 %collective-permute-start.17 = (bf16[256,1024]{1,0:T(8,128)(2,1)}, bf16[256,1024]{1,0:T(8,128)(2,1)}, u32[]{:S(2)}, u32[]{:S(2)}) collective-permute-start(bf16[256,1024]{1,0:T(8,128)(2,1)} %get-tuple-element.87), channel_id=1, source_target_pairs={{0,2},{1,3},{2,4},{3,5},{4,6},{5,7},{8,10},{9,11},{10,12},{11,13},... | collective-permute-start | bytes 1572872 | tf_op jit(solution)/shard_map/ppermute | solution.py:480
  101.3 1.5 collective-permute-start.18
  102.8 1.0 add_bitcast_fusion
  104.1 0.6 fusion.1
  106.0 1.6 pad_maximum_fusion.2
  107.6 2.6 %copy.13 = bf16[27,64,256]{2,1,0:T(8,128)(2,1)} copy(bf16[27,64,256]{1,2,0:T(8,128)(2,1)} %pad_maximum_fusion.2) | data formatting | bytes 1769472 | tf_op jit(solution)/shard_map/concatenate | solution.py:531
  110.2 1.5 copy.14
  111.7 3.7 %pad_maximum_fusion.weights_ref = bf16[2,2,4,2,7,32,256]{6,5,4,3,2,1,0:T(8,128)(2,1)} fusion(bf16[1,2,4,2,7,32,256]{6,5,4,3,2,1,0:T(8,128)(2,1)} %copy-done, bf16[1,2,4,2,7,32,256]{6,5,4,3,2,1,0:T(8,128)(2,1)S(1)} %get-tuple-element.82), kind=kLoop, calls=%fused_computation.1 | loop fusion | flops 1835008 | bytes 7340032 | tf_op jit(solution)/shard_map/stack | solution.py:437
  115.4 1.9 %collective-permute-done.18.above_ref = bf16[256,1024]{1,0:T(8,128)(2,1)} collective-permute-done((bf16[256,1024]{1,0:T(8,128)(2,1)S(1)}, bf16[256,1024]{1,0:T(8,128)(2,1)}, u32[]{:S(2)}, u32[]{:S(2)}) %collective-permute-start.18) | collective-permute-done | bytes 524320 | tf_op jit(solution)/shard_map/ppermute | solution.py:480
  117.9 9.0 %input_part.2 = f32[256,1024]{1,0:T(8,128)} custom-call(s32[1]{0:T(128)S(6)} %sub.33.which_ref, bf16[256,1024]{1,0:T(8,128)(2,1)} %collective-permute-done.17.below_ref, bf16[256,2048]{1,0:T(8,128)(2,1)} %bitcast.81, bf16[256,1024]{1,0:T(8,128)(2,1)} %collective-permute-done.18.above_ref, bf16[2,2,4,2,7,32,256]{6,5,4,3,2,1,0:T(8,128)(2,1)} %pad_maximum_fusion.weights_ref), custom_call_target="tpu_custom_call" | custom-call | flops 3623878656 | bytes 8388608 | tf_op jit(solution)/shard_map/input_part/pallas_call | solution.py:344
  127.0 2.3 %collective-permute-done.21 = f32[8,8,1792]{2,1,0:T(8,128)S(1)} collective-permute-done((f32[8,8,1792]{2,1,0:T(8,128)S(1)}, f32[8,8,1792]{2,1,0:T(8,128)S(1)}, u32[]{:S(2)}, u32[]{:S(2)}) %collective-permute-start.21) | collective-permute-done | bytes 458784 | tf_op jit(solution)/shard_map/ppermute | solution.py:480
  129.2 0.8 bitcast_add_fusion
  130.1 3.5 %all-to-all-start = ((f32[8,8,1792]{2,1,0:T(8,128)}), f32[8,8,1792]{2,1,0:T(8,128)S(1)}, u32[]{:S(2)}, u32[]{:S(2)}) async-start(f32[8,8,1792]{2,1,0:T(8,128)} %bitcast_add_fusion), calls=%async_computation | async-start | bytes 917504 | tf_op jit(solution)/shard_map/all_to_all | solution.py:543
  133.6 2.0 %collective-permute-start.23 = (f32[256,1024]{1,0:T(8,128)}, f32[256,1024]{1,0:T(8,128)S(1)}, u32[]{:S(2)}, u32[]{:S(2)}) collective-permute-start(f32[256,1024]{1,0:T(8,128)} %input_part.2), channel_id=1, source_target_pairs={{0,1},{1,0},{2,3},{3,2},{4,5},{5,4},{6,7},{7,6},{8,9},{9,8},{10,11... | collective-permute-start | bytes 3145736 | tf_op jit(solution)/shard_map/ppermute | solution.py:480
  135.6 0.7 copy.18.refs_9_
  136.3 0.6 stack.181.place_ref
  136.9 1.3 copy.17.refs_8_
  138.2 7.8 %all-to-all-done = f32[8,8,1792]{2,1,0:T(8,128)S(1)} async-done(((f32[8,8,1792]{2,1,0:T(8,128)}), f32[8,8,1792]{2,1,0:T(8,128)S(1)}, u32[]{:S(2)}, u32[]{:S(2)}) %all-to-all-start) | async-done | bytes 458784 | tf_op jit(solution)/shard_map/all_to_all | solution.py:543
  146.5 11.9 %forward.1 = bf16[64,8192]{1,0:T(8,128)(2,1)} custom-call(s32[8]{0:T(128)} %stack.181.place_ref, bf16[256,1024]{1,0:T(8,128)(2,1)} %bitcast.96, bf16[256,1024]{1,0:T(8,128)(2,1)} %copy-done.12, bf16[256,1024]{1,0:T(8,128)(2,1)} %copy-done.7, bf16[256,1024]{1,0:T(8,128)(2,1)} %copy-done.8, bf16[256,1024]{1,0:T(8,128)(2,1)} %copy-done.13, ...), custom_call_target="tpu_custom_call" | custom-call | flops 7247757312 | bytes 6291456 | tf_op jit(solution)/shard_map/forward/pallas_call | solution.py:186
  158.4 8.9 %input_part.3 = f32[256,1024]{1,0:T(8,128)} custom-call(s32[1]{0:T(128)} %bitcast.1.which_ref, bf16[256,1024]{1,0:T(8,128)(2,1)} %collective-permute-done.17.below_ref, bf16[256,2048]{1,0:T(8,128)(2,1)} %bitcast.82, bf16[256,1024]{1,0:T(8,128)(2,1)} %collective-permute-done.18.above_ref, bf16[2,2,4,2,7,32,256]{6,5,4,3,2,1,0:T(8,128)(2,1)} %pad_maximum_fusion.weights_ref), custom_call_target="tpu_custom_call" | custom-call | flops 3623878656 | bytes 8388608 | tf_op jit(solution)/shard_map/input_part/pallas_call | solution.py:344
  168.9 2.1 %fusion.2 = bf16[1,256,1024]{2,1,0:T(8,128)(2,1)} fusion(f32[256,1024]{1,0:T(8,128)} %input_part.3, f32[256,1024]{1,0:T(8,128)S(1)} %collective-permute-done.23), kind=kLoop, calls=%fused_computation.14 | loop fusion | flops 524288 | bytes 2621440 | tf_op jit(solution)/shard_map/broadcast_in_dim | solution.py:557
  171.0 3.3 %arrange.1 = f32[27,32,512]{2,1,0:T(8,128)} custom-call(f32[1]{0:T(128)} %copy.35.scale_ref, s32[1]{0:T(128)} %bitcast.2.core_ref, f32[2,8,8,1792]{3,2,1,0:T(8,128)} %copy-done.2, f32[2,8,8,1792]{3,2,1,0:T(8,128)} %collective-permute-done.24.other_ref), custom_call_target="tpu_custom_call" | custom-call | tf_op jit(solution)/shard_map/arrange/pallas_call | solution.py:422
  (93 shorter events, 9.5 us)
Async XLA Ops:
  0.6 19.9 %collective-permute-start = (bf16[256,1024]{1,0:T(8,128)(2,1)}, bf16[256,1024]{1,0:T(8,128)(2,1)S(1)}, u32[]{:S(2)}, u32[]{:S(2)}) collective-permute-start(bf16[256,1024]{1,0:T(8,128)(2,1)} %bitcast.92), channel_id=1, source_target_pairs={{0,2},{1,3},{2,0},{3,1},{4,6},{5,7},{6,4},{7,5},{8,10},{9,11},{10,... | collective-permute-start | bytes 1572872 | tf_op jit(solution)/shard_map/ppermute | solution.py:480
  3.7 16.8 %collective-permute-start.1 = (bf16[256,1024]{1,0:T(8,128)(2,1)}, bf16[256,1024]{1,0:T(8,128)(2,1)S(1)}, u32[]{:S(2)}, u32[]{:S(2)}) collective-permute-start(bf16[256,1024]{1,0:T(8,128)(2,1)} %bitcast.93), channel_id=1, source_target_pairs={{2,4},{3,5},{4,2},{5,3},{10,12},{11,13},{12,10},{13,11},{18,20},{1... | collective-permute-start | bytes 1572872 | tf_op jit(solution)/shard_map/ppermute | solution.py:480
  4.4 16.1 %collective-permute-start.2 = (bf16[256,1024]{1,0:T(8,128)(2,1)}, bf16[256,1024]{1,0:T(8,128)(2,1)S(1)}, u32[]{:S(2)}, u32[]{:S(2)}) collective-permute-start(bf16[256,1024]{1,0:T(8,128)(2,1)} %bitcast.94), channel_id=1, source_target_pairs={{0,1},{1,0},{2,3},{3,2},{4,5},{5,4},{6,7},{7,6},{8,9},{9,8},{10,11... | collective-permute-start | bytes 1572872 | tf_op jit(solution)/shard_map/ppermute | solution.py:480
  8.6 12.0 %collective-permute-start.3 = (bf16[7,32,256]{2,1,0:T(8,128)(2,1)}, bf16[7,32,256]{2,1,0:T(8,128)(2,1)S(1)}, u32[]{:S(2)}, u32[]{:S(2)}) collective-permute-start(bf16[7,32,256]{2,1,0:T(8,128)(2,1)} %get-tuple-element.43), channel_id=1, source_target_pairs={{0,1},{1,0},{2,3},{3,2},{4,5},{5,4},{6,7},{7,6},{8,9},{9,8},{10,11... | collective-permute-start | bytes 344072 | tf_op jit(solution)/shard_map/ppermute | solution.py:480
  20.5 9.7 %copy-start.12 = (bf16[256,1024]{1,0:T(8,128)(2,1)}, bf16[256,1024]{1,0:T(8,128)(2,1)S(1)}, u32[]{:S(2)}) copy-start(bf16[256,1024]{1,0:T(8,128)(2,1)S(1)} %collective-permute-done.near_ref.refs_1_) | copy-start | bytes 1572868
  20.5 4.2 %copy-start.13 = (bf16[256,1024]{1,0:T(8,128)(2,1)}, bf16[256,1024]{1,0:T(8,128)(2,1)S(1)}, u32[]{:S(2)}) copy-start(bf16[256,1024]{1,0:T(8,128)(2,1)S(1)} %collective-permute-done.2.far_ref.refs_4_) | copy-start | bytes 1572868
  20.6 9.7 %collective-permute-start.4 = (bf16[256,1024]{1,0:T(8,128)(2,1)S(1)}, bf16[256,1024]{1,0:T(8,128)(2,1)S(1)}, u32[]{:S(2)}, u32[]{:S(2)}) collective-permute-start(bf16[256,1024]{1,0:T(8,128)(2,1)S(1)} %collective-permute-done.near_ref.refs_1_), channel_id=1, source_target_pairs={{2,4},{3,5},{4,2},{5,3},{10,12},{11,13},{12,10},{13,11},{18,20},{1... | collective-permute-start | bytes 1572872 | tf_op jit(solution)/shard_map/ppermute | solution.py:480
  21.3 17.3 %collective-permute-start.5 = (bf16[256,1024]{1,0:T(8,128)(2,1)S(1)}, bf16[256,1024]{1,0:T(8,128)(2,1)S(1)}, u32[]{:S(2)}, u32[]{:S(2)}) collective-permute-start(bf16[256,1024]{1,0:T(8,128)(2,1)S(1)} %collective-permute-done.1), channel_id=1, source_target_pairs={{2,0},{3,1},{4,6},{5,7},{10,8},{11,9},{12,14},{13,15},{18,16},{19,... | collective-permute-start | bytes 1572872 | tf_op jit(solution)/shard_map/ppermute | solution.py:480
  22.6 16.0 %collective-permute-start.6 = (bf16[256,1024]{1,0:T(8,128)(2,1)S(1)}, bf16[256,1024]{1,0:T(8,128)(2,1)}, u32[]{:S(2)}, u32[]{:S(2)}) collective-permute-start(bf16[256,1024]{1,0:T(8,128)(2,1)S(1)} %collective-permute-done.near_ref.refs_1_), channel_id=1, source_target_pairs={{0,1},{1,0},{2,3},{3,2},{4,5},{5,4},{6,7},{7,6},{8,9},{9,8},{10,11... | collective-permute-start | bytes 1572872 | tf_op jit(solution)/shard_map/ppermute | solution.py:480
  24.7 16.8 %copy-start.9 = (bf16[7,32,256]{2,1,0:T(8,128)(2,1)S(1)}, bf16[7,32,256]{2,1,0:T(8,128)(2,1)}, u32[]{:S(2)}) copy-start(bf16[7,32,256]{2,1,0:T(8,128)(2,1)} %get-tuple-element.51) | copy-start | bytes 344068
  38.6 15.3 %copy-start.7 = (bf16[256,1024]{1,0:T(8,128)(2,1)}, bf16[256,1024]{1,0:T(8,128)(2,1)S(1)}, u32[]{:S(2)}) copy-start(bf16[256,1024]{1,0:T(8,128)(2,1)S(1)} %broadcast_select_fusion.1.near_ref.refs_2_) | copy-start | bytes 1572868
  38.7 29.5 %collective-permute-start.8 = (bf16[256,1024]{1,0:T(8,128)(2,1)S(1)}, bf16[256,1024]{1,0:T(8,128)(2,1)S(1)}, u32[]{:S(2)}, u32[]{:S(2)}) collective-permute-start(bf16[256,1024]{1,0:T(8,128)(2,1)S(1)} %broadcast_select_fusion.1.near_ref.refs_2_), channel_id=1, source_target_pairs={{0,1},{1,0},{2,3},{3,2},{4,5},{5,4},{6,7},{7,6},{8,9},{9,8},{10,11... | collective-permute-start | bytes 1572872 | tf_op jit(solution)/shard_map/ppermute | solution.py:480
  40.2 27.9 %collective-permute-start.7 = (bf16[256,1024]{1,0:T(8,128)(2,1)S(1)}, bf16[256,1024]{1,0:T(8,128)(2,1)S(1)}, u32[]{:S(2)}, u32[]{:S(2)}) collective-permute-start(bf16[256,1024]{1,0:T(8,128)(2,1)S(1)} %collective-permute-done.4), channel_id=1, source_target_pairs={{2,0},{3,1},{4,6},{5,7},{10,8},{11,9},{12,14},{13,15},{18,16},{19,... | collective-permute-start | bytes 1572872 | tf_op jit(solution)/shard_map/ppermute | solution.py:480
  41.6 17.8 %collective-permute-start.10 = (bf16[2,7,32,256]{3,2,1,0:T(8,128)(2,1)S(1)}, bf16[2,7,32,256]{3,2,1,0:T(8,128)(2,1)S(1)}, u32[]{:S(2)}, u32[]{:S(2)}) collective-permute-start(bf16[2,7,32,256]{3,2,1,0:T(8,128)(2,1)S(1)} %pad_maximum_fusion.4), channel_id=1, source_target_pairs={{0,4},{1,5},{2,6},{3,7},{4,0},{5,1},{6,2},{7,3},{8,12},{9,13},{10,... | collective-permute-start | bytes 688136 | tf_op jit(solution)/shard_map/ppermute | solution.py:480
  45.2 22.9 %collective-permute-start.11 = (bf16[2,7,32,256]{3,2,1,0:T(8,128)(2,1)S(1)}, bf16[2,7,32,256]{3,2,1,0:T(8,128)(2,1)S(1)}, u32[]{:S(2)}, u32[]{:S(2)}) collective-permute-start(bf16[2,7,32,256]{3,2,1,0:T(8,128)(2,1)S(1)} %pad_maximum_fusion.4), channel_id=1, source_target_pairs={{0,6},{1,7},{2,0},{3,1},{4,2},{5,3},{6,4},{7,5},{8,14},{9,15},{10,... | collective-permute-start | bytes 688136 | tf_op jit(solution)/shard_map/ppermute | solution.py:480
  46.7 21.4 %collective-permute-start.9 = (bf16[2,7,32,256]{3,2,1,0:T(8,128)(2,1)S(1)}, bf16[2,7,32,256]{3,2,1,0:T(8,128)(2,1)S(1)}, u32[]{:S(2)}, u32[]{:S(2)}) collective-permute-start(bf16[2,7,32,256]{3,2,1,0:T(8,128)(2,1)S(1)} %pad_maximum_fusion.4), channel_id=1, source_target_pairs={{0,2},{1,3},{2,4},{3,5},{4,6},{5,7},{6,0},{7,1},{8,10},{9,11},{10,... | collective-permute-start | bytes 688136 | tf_op jit(solution)/shard_map/ppermute | solution.py:480
  68.1 0.8 copy-start.14
  68.3 3.4 %copy-start.5 = (bf16[1,64,8192]{2,1,0:T(8,128)(2,1)S(1)}, bf16[1,64,8192]{2,1,0:T(8,128)(2,1)}, u32[]{:S(2)}) copy-start(bf16[1,64,8192]{2,1,0:T(8,128)(2,1)} %param.8) | copy-start | bytes 3145732
  68.9 22.0 %collective-permute-start.13 = (bf16[4,2,7,32,256]{4,3,2,1,0:T(8,128)(2,1)S(1)}, bf16[4,2,7,32,256]{4,3,2,1,0:T(8,128)(2,1)S(1)}, u32[]{:S(2)}, u32[]{:S(2)}) collective-permute-start(bf16[4,2,7,32,256]{4,3,2,1,0:T(8,128)(2,1)S(1)} %constant_dynamic-slice_fusion.5), channel_id=1, source_target_pairs={{0,16},{8,24},{16,0},{24,8},{1,17},{9,25},{17,1},{25,9},{2,18},{10... | collective-permute-start | bytes 2752520 | tf_op jit(solution)/shard_map/ppermute | solution.py:480
  70.5 11.3 %copy-start.8 = (bf16[256,1024]{1,0:T(8,128)(2,1)}, bf16[256,1024]{1,0:T(8,128)(2,1)S(1)}, u32[]{:S(2)}) copy-start(bf16[256,1024]{1,0:T(8,128)(2,1)S(1)} %broadcast_select_fusion.near_ref.refs_3_) | copy-start | bytes 1572868
  70.5 11.7 %collective-permute-start.12 = (bf16[256,1024]{1,0:T(8,128)(2,1)S(1)}, bf16[256,1024]{1,0:T(8,128)(2,1)S(1)}, u32[]{:S(2)}, u32[]{:S(2)}) collective-permute-start(bf16[256,1024]{1,0:T(8,128)(2,1)S(1)} %broadcast_select_fusion.near_ref.refs_3_), channel_id=1, source_target_pairs={{0,1},{1,0},{2,3},{3,2},{4,5},{5,4},{6,7},{7,6},{8,9},{9,8},{10,11... | collective-permute-start | bytes 1572872 | tf_op jit(solution)/shard_map/ppermute | solution.py:480
  71.8 17.7 %collective-permute-start.14 = (bf16[64,2048]{1,0:T(8,128)(2,1)S(1)}, bf16[64,2048]{1,0:T(8,128)(2,1)S(1)}, u32[]{:S(2)}, u32[]{:S(2)}) collective-permute-start(bf16[64,2048]{1,0:T(8,128)(2,1)S(1)} %get-tuple-element.90), channel_id=1, source_target_pairs={{0,2},{1,3},{2,4},{3,5},{4,6},{5,7},{6,0},{7,1},{8,10},{9,11},{10,... | collective-permute-start | bytes 786440 | tf_op jit(solution)/shard_map/ppermute | solution.py:480
  71.9 19.0 %collective-permute-start.15 = (bf16[64,2048]{1,0:T(8,128)(2,1)S(1)}, bf16[64,2048]{1,0:T(8,128)(2,1)S(1)}, u32[]{:S(2)}, u32[]{:S(2)}) collective-permute-start(bf16[64,2048]{1,0:T(8,128)(2,1)S(1)} %get-tuple-element.89), channel_id=1, source_target_pairs={{0,4},{1,5},{2,6},{3,7},{4,0},{5,1},{6,2},{7,3},{8,12},{9,13},{10,... | collective-permute-start | bytes 786440 | tf_op jit(solution)/shard_map/ppermute | solution.py:480
  74.5 16.4 %collective-permute-start.16 = (bf16[64,2048]{1,0:T(8,128)(2,1)S(1)}, bf16[64,2048]{1,0:T(8,128)(2,1)S(1)}, u32[]{:S(2)}, u32[]{:S(2)}) collective-permute-start(bf16[64,2048]{1,0:T(8,128)(2,1)S(1)} %get-tuple-element.88), channel_id=1, source_target_pairs={{0,6},{1,7},{2,0},{3,1},{4,2},{5,3},{6,4},{7,5},{8,14},{9,15},{10,... | collective-permute-start | bytes 786440 | tf_op jit(solution)/shard_map/ppermute | solution.py:480
  82.2 0.8 copy-start.15
  91.0 1.2 copy-start.11
  91.2 12.6 %collective-permute-start.20 = (bf16[2,4,2,7,32,256]{5,4,3,2,1,0:T(8,128)(2,1)S(1)}, bf16[2,4,2,7,32,256]{5,4,3,2,1,0:T(8,128)(2,1)S(1)}, u32[]{:S(2)}, u32[]{:S(2)}) collective-permute-start(bf16[2,4,2,7,32,256]{5,4,3,2,1,0:T(8,128)(2,1)S(1)} %pad_maximum_fusion.1), channel_id=1, source_target_pairs={{0,8},{8,0},{16,24},{24,16},{1,9},{9,1},{17,25},{25,17},{2,10},{10... | collective-permute-start | bytes 5505032 | tf_op jit(solution)/shard_map/ppermute | solution.py:480
  92.2 10.6 %collective-permute-start.19 = (f32[8,16,1792]{2,1,0:T(8,128)S(1)}, f32[8,16,1792]{2,1,0:T(8,128)S(1)}, u32[]{:S(2)}, u32[]{:S(2)}) collective-permute-start(f32[8,16,1792]{2,1,0:T(8,128)S(1)} %copy-done.11), channel_id=1, source_target_pairs={{0,8},{8,0},{16,24},{24,16},{1,9},{9,1},{17,25},{25,17},{2,10},{10... | collective-permute-start | bytes 2752520 | tf_op jit(solution)/shard_map/ppermute | solution.py:480
  92.4 10.4 %copy-start.6 = (f32[8,16,1792]{2,1,0:T(8,128)S(1)}, f32[8,16,1792]{2,1,0:T(8,128)}, u32[]{:S(2)}) copy-start(f32[8,16,1792]{2,1,0:T(8,128)} %get-tuple-element.67) | copy-start | bytes 2752516
  92.5 11.3 %copy-start.1 = (bf16[4,64,2048]{2,1,0:T(8,128)(2,1)}, bf16[4,64,2048]{2,1,0:T(8,128)(2,1)S(1)}, u32[]{:S(2)}) copy-start(bf16[4,64,2048]{2,1,0:T(8,128)(2,1)S(1)} %constant_dynamic-slice_fusion) | copy-start | bytes 3145732
  93.4 22.1 %collective-permute-start.17 = (bf16[256,1024]{1,0:T(8,128)(2,1)}, bf16[256,1024]{1,0:T(8,128)(2,1)}, u32[]{:S(2)}, u32[]{:S(2)}) collective-permute-start(bf16[256,1024]{1,0:T(8,128)(2,1)} %get-tuple-element.87), channel_id=1, source_target_pairs={{0,2},{1,3},{2,4},{3,5},{4,6},{5,7},{8,10},{9,11},{10,12},{11,13},... | collective-permute-start | bytes 1572872 | tf_op jit(solution)/shard_map/ppermute | solution.py:480
  101.3 16.0 %collective-permute-start.18 = (bf16[256,1024]{1,0:T(8,128)(2,1)S(1)}, bf16[256,1024]{1,0:T(8,128)(2,1)}, u32[]{:S(2)}, u32[]{:S(2)}) collective-permute-start(bf16[256,1024]{1,0:T(8,128)(2,1)S(1)} %get-tuple-element.86), channel_id=1, source_target_pairs={{2,0},{3,1},{4,2},{5,3},{6,4},{7,5},{10,8},{11,9},{12,10},{13,11},... | collective-permute-start | bytes 1572872 | tf_op jit(solution)/shard_map/ppermute | solution.py:480
  104.1 1.2 copy-start
  111.7 5.6 %copy-start.3 = (f32[8,2,8,1792]{3,2,1,0:T(8,128)S(1)}, f32[8,2,8,1792]{3,2,1,0:T(8,128)}, u32[]{:S(2)}) copy-start(f32[8,2,8,1792]{3,2,1,0:T(8,128)} %add_bitcast_fusion) | copy-start | bytes 2752516
  117.3 11.9 %collective-permute-start.21 = (f32[8,8,1792]{2,1,0:T(8,128)S(1)}, f32[8,8,1792]{2,1,0:T(8,128)S(1)}, u32[]{:S(2)}, u32[]{:S(2)}) collective-permute-start(f32[8,8,1792]{2,1,0:T(8,128)S(1)} %dynamic-slice_bitcast_fusion), channel_id=1, source_target_pairs={{0,16},{8,24},{16,0},{24,8},{1,17},{9,25},{17,1},{25,9},{2,18},{10... | collective-permute-start | bytes 1376264 | tf_op jit(solution)/shard_map/ppermute | solution.py:480
  117.9 11.3 %copy-start.4 = (f32[8,2,8,1792]{3,2,1,0:T(8,128)S(1)}, f32[8,2,8,1792]{3,2,1,0:T(8,128)}, u32[]{:S(2)}) copy-start(f32[8,2,8,1792]{3,2,1,0:T(8,128)} %add_bitcast_fusion) | copy-start | bytes 2752516
  126.9 8.7 %copy-start.10 = (f32[64]{0:T(128)S(1)}, f32[64]{0:T(128)}, u32[]{:S(2)}) copy-start(f32[64]{0:T(128)} %param.7) | copy-start | bytes 772
  130.1 15.9 %all-to-all-start = ((f32[8,8,1792]{2,1,0:T(8,128)}), f32[8,8,1792]{2,1,0:T(8,128)S(1)}, u32[]{:S(2)}, u32[]{:S(2)}) async-start(f32[8,8,1792]{2,1,0:T(8,128)} %bitcast_add_fusion), calls=%async_computation | async-start | bytes 917504 | tf_op jit(solution)/shard_map/all_to_all | solution.py:543
  133.6 33.8 %collective-permute-start.23 = (f32[256,1024]{1,0:T(8,128)}, f32[256,1024]{1,0:T(8,128)S(1)}, u32[]{:S(2)}, u32[]{:S(2)}) collective-permute-start(f32[256,1024]{1,0:T(8,128)} %input_part.2), channel_id=1, source_target_pairs={{0,1},{1,0},{2,3},{3,2},{4,5},{5,4},{6,7},{7,6},{8,9},{9,8},{10,11... | collective-permute-start | bytes 3145736 | tf_op jit(solution)/shard_map/ppermute | solution.py:480
  145.9 21.4 %collective-permute-start.22 = (f32[8,8,1792]{2,1,0:T(8,128)S(1)}, f32[8,8,1792]{2,1,0:T(8,128)S(1)}, u32[]{:S(2)}, u32[]{:S(2)}) collective-permute-start(f32[8,8,1792]{2,1,0:T(8,128)S(1)} %all-to-all-done), channel_id=1, source_target_pairs={{0,16},{8,24},{16,0},{24,8},{1,17},{9,25},{17,1},{25,9},{2,18},{10... | collective-permute-start | bytes 1376264 | tf_op jit(solution)/shard_map/ppermute | solution.py:480
  167.5 3.5 %copy-start.2 = (f32[2,8,8,1792]{3,2,1,0:T(8,128)}, f32[2,8,8,1792]{3,2,1,0:T(8,128)S(1)}, u32[]{:S(2)}) copy-start(f32[2,8,8,1792]{3,2,1,0:T(8,128)S(1)} %pad_maximum_fusion.3.own_ref) | copy-start | bytes 2752516
  167.5 3.5 %collective-permute-start.24 = (f32[2,8,8,1792]{3,2,1,0:T(8,128)S(1)}, f32[2,8,8,1792]{3,2,1,0:T(8,128)}, u32[]{:S(2)}, u32[]{:S(2)}) collective-permute-start(f32[2,8,8,1792]{3,2,1,0:T(8,128)S(1)} %pad_maximum_fusion.3.own_ref), channel_id=1, source_target_pairs={{0,8},{8,0},{16,24},{24,16},{1,9},{9,1},{17,25},{25,17},{2,10},{10... | collective-permute-start | bytes 2752520 | tf_op jit(solution)/shard_map/ppermute | solution.py:480

commit v3 on v2

--- a/solution.py
+++ b/solution.py
@@ -296,7 +296,7 @@
 
 
 def input_kernel(
-    which_ref, below_ref, middle_ref, above_ref, weights_ref, out_ref,
+    place_ref, below_ref, middle_ref, above_ref, own_ref, other_ref, upper_ref, lower_ref,
     planes_ref, kernel_ref, even_ref, odd_ref, sems,
 ):
     filters = below_ref.shape[0]
@@ -305,19 +305,17 @@
     for part in range(parts):
         copies.append([])
         for index in range(8):
-            quarter, x = index // 2, index % 2
-            to_ref = kernel_ref.at[part, pl.ds(7 * quarter, 7), pl.ds(32 * x, 32), :]
-            copies[-1].append(
-                pltpu.make_async_copy(
-                    weights_ref.at[quarter % 2, quarter // 2, part, x], to_ref, sems.at[part, index]
-                )
-            )
+            away, y, x = index // 4, index // 2 % 2, index % 2
+            core = 1 - place_ref[1] if away else place_ref[1]
+            from_ref = (other_ref if away else own_ref).at[y, part, x]
+            to_ref = kernel_ref.at[part, pl.ds(7 * (2 * y + core), 7), pl.ds(32 * x, 32), :]
+            copies[-1].append(pltpu.make_async_copy(from_ref, to_ref, sems.at[part, index]))
             copies[-1][-1].start()
     planes_ref[:filters, :] = below_ref[...]
     planes_ref[filters : 2 * filters, :] = middle_ref[:, :PLANE]
     planes_ref[2 * filters : 3 * filters, :] = middle_ref[:, PLANE:]
     planes_ref[3 * filters :, :] = above_ref[...]
-    start = pl.multiple_of(which_ref[0] * filters, filters)
+    start = pl.multiple_of(place_ref[0] * filters, filters)
 
     def multiply(part, into_ref):
         for copy in copies[part]:
@@ -332,12 +330,14 @@
         )
 
     def finish(part, from_ref):
-        out_ref[part * rows : (part + 1) * rows, :] = gather_shifts(from_ref, rows, -1)
+        out_ref = upper_ref if part < parts // 2 else lower_ref
+        start = part % (parts // 2) * rows
+        out_ref[start : start + rows, :] = gather_shifts(from_ref, rows, -1)
 
     in_turn(multiply, finish, (even_ref, odd_ref), parts)
 
 
-def input_part(which, below, middle, above, kernel, rows=64):
+def input_part(place, below, middle, above, own, other, rows=64):
     filters, cells = below.shape
     channels = 4 * rows
     vmem = pl.BlockSpec(memory_space=pltpu.VMEM)
@@ -349,9 +349,10 @@
             vmem,
             vmem,
             pl.BlockSpec(memory_space=pl.ANY),
+            pl.BlockSpec(memory_space=pl.ANY),
         ],
-        out_specs=vmem,
-        out_shape=jax.ShapeDtypeStruct((channels, cells), jnp.float32),
+        out_specs=[vmem, vmem],
+        out_shape=[jax.ShapeDtypeStruct((channels // 2, cells), jnp.float32)] * 2,
         scratch_shapes=[
             pltpu.VMEM((4 * filters, cells), jnp.bfloat16),
             pltpu.VMEM((channels // rows, 28, rows, filters), jnp.bfloat16),
@@ -366,7 +367,7 @@
             transcendentals=0,
         ),
         name="input_part",
-    )(which, below, middle, above, kernel)
+    )(place, below, middle, above, own, other)
 
 
 def pick_kernel(place_ref, weights_ref, own_ref, other_ref):
@@ -493,21 +494,21 @@
     first_tap = jnp.minimum(7 * (2 * y + core), TAPS - 7)
     keep, give = pick(jnp.stack([first_tap, x]).astype(jnp.int32), weights, 7)
     given = along(give, "sp", "swap_x")
-    second, third, own_far, given = together((second, third, own_far, given))
+    second, third, own_far = together((second, third, own_far))
 
     near, far = [own], [own_far]
     fourth = along(second, "sp", "cross_z")
     third_out = along(third, "sp", "out_z")
     near.append(second)
     far.append(along(second, "sp", "swap_x"))
-    kernel = in_order(keep, given, x)
-    ring = [kernel] + [along(kernel, "sp", f"turn_z{k}") for k in (1, 2, 3)]
     part = add_pair(0, None)
-    fourth, third_out, far[1], part = together((fourth, third_out, far[1], part))
+    fourth, third_out, far[1], part, given = together((fourth, third_out, far[1], part, given))
 
     near.append(jnp.where(inner, third, third_out))
     far.append(along(near[2], "sp", "swap_x"))
     fourth_out = along(fourth, "sp", "out_z")
+    kernel = in_order(keep, given, x)
+    ring = [kernel] + [along(kernel, "sp", f"turn_z{k}") for k in (1, 2, 3)]
     part = add_pair(1, part)
     fourth_out, far[2], part, *ring = together((fourth_out, far[2], part, *ring))
 
@@ -525,35 +526,40 @@
     above = along(middle[:, :PLANE], "sp", "down_z")
     given = along(give, "grp", "swap_core")
     kernel = in_order(kernel, arrived, y)
-    kernel = in_order(kernel, along(kernel, "grp", "swap_core"), core)
-    own_filters = lax.dynamic_slice_in_dim(kernel, z * 64, 64, 6)
+    other_kernel = along(kernel, "grp", "swap_core")
+    own_filters = in_order(
+        lax.dynamic_slice_in_dim(kernel, z * 64, 64, 5),
+        lax.dynamic_slice_in_dim(other_kernel, z * 64, 64, 5),
+        core,
+    )
     own_filters = own_filters.transpose(1, 0, 4, 6, 2, 3, 5).reshape(28, 64, 256)
     own_filters = jnp.concatenate([own_filters[:21], own_filters[22:]])
     own_filters = own_filters.reshape(3, 9 * 64, 256).transpose(1, 0, 2).reshape(9 * 64, 3 * 256)
     width = rows.shape[2]
     rows = (rows + given).reshape(8, 2, 8, width)
-    below, above, rows, kernel, own_filters = together((below, above, rows, kernel, own_filters))
-
     arrived = along(half(rows, 1, 1 - y), "grp", "swap_y")
-    which = x.astype(jnp.int32)[None]
-    other_plane = input_part(1 - which, below, middle, above, kernel)
-    arrived, other_plane = together((arrived, other_plane))
-
-    other_plane = along(other_plane, "sp", "swap_x")
+    below, above, other_kernel, own_filters = together(
+        (below, above, other_kernel, own_filters)
+    )
+
     rows = lax.all_to_all(half(rows, 1, y) + arrived, "sp", 0, 0)
+    planes = below, middle, above, kernel, other_kernel
+    upper, lower = input_part(jnp.stack([1 - x, core]).astype(jnp.int32), *planes)
+    upper = along(upper, "sp", "swap_x")
     place = jnp.stack([2 * s + x for s in sources] + [2 * s + 1 - x for s in sources])
     conv_out = forward(place.astype(jnp.int32), near + far, own_filters, conv_bias)
-    own_plane = input_part(which, below, middle, above, kernel)
+    rows, upper, lower, conv_out = together((rows, upper, lower, conv_out))
+
+    lower = along(lower, "sp", "swap_x")
     arrived = along(rows, "grp", "swap_y")
-    rows, arrived, other_plane, own_plane, conv_out = together(
-        (rows, arrived, other_plane, own_plane, conv_out)
-    )
+    own_planes = input_part(jnp.stack([x, core]).astype(jnp.int32), *planes)
+    arrived, lower, own_planes = together((arrived, lower, own_planes))
 
     rows = in_order(rows, arrived, y)
     other_rows = along(rows, "grp", "swap_core")
     grad_weight = arrange(loss_scale, core.astype(jnp.int32)[None], rows, other_rows)
     bias_sum = half(rows[0], 0, lax.axis_index("sp"))[0, TAPS * 64 :]
-    grad_input = (own_plane + other_plane).astype(jnp.bfloat16)
+    grad_input = jnp.concatenate([own_planes[0] + upper, own_planes[1] + lower]).astype(jnp.bfloat16)
     return (conv_out[None], grad_input[None], grad_weight, bias_sum / loss_scale[0])
 
 

time: 175 us -> 166 us (0.949)
  waiting for transfers between devices: 47.5 us -> 35.9 us
  starting transfers between devices: 40.1 us -> 47.9 us
  other arithmetic: 13.7 us -> 10.1 us
    all_to_all x1, waiting for transfers between devices: 7.75 us -> 0.01 us  [per_device(): rows = lax.all_to_all(half(rows, 1, y) + arrived, 'sp', 0, 0)]
    ppermute x25 -> x26, starting transfers between devices: 36.5 us -> 41.4 us  [along(): return lax.ppermute(value, axis, at[steps])]
    ppermute x25 -> x26, waiting for transfers between devices: 39.8 us -> 35.9 us  [along(): return lax.ppermute(value, axis, at[steps])]
    all_to_all x1, starting transfers between devices: 3.53 us -> 6.47 us  [per_device(): rows = lax.all_to_all(half(rows, 1, y) + arrived, 'sp', 0, 0)]
    broadcast_in_dim x1 -> x0, other arithmetic: 2.14 us -> none  [per_device(): grad_input[None]]
    unnamed x44 -> x42, local copies, waits for them, and re-layouts: 3.05 us -> 3.83 us
    another operation x7 -> x6, other arithmetic: 4.36 us -> 3.69 us  [in_order(): jnp.stack([jnp.where(bit == 0, own, other), jnp.where(bit == 0, other, ow...]
  transfers between devices with their start and end apart: 26 -> 27, of which waited for: 9 -> 11; matrix products, arithmetic and copies ran while one was open for 12% -> 10% of each run, Pallas kernels for 32% -> 34%
where the time goes in v3:
time: 166 us
  Pallas kernels  59.3 us (36%)
  starting transfers between devices  47.9 us (29%)
  waiting for transfers between devices  35.9 us (22%)
  local copies, waits for them, and re-layouts  10.8 us (7%)
  other arithmetic  10.1 us (6%)
  between operations  1.78 us (1%)
    ppermute x26, starting transfers between devices, along(): return lax.ppermute(value, axis, at[steps])  41.4 us
    ppermute x26, waiting for transfers between devices, along(): return lax.ppermute(value, axis, at[steps])  35.9 us
    pallas_call x4, Pallas kernels, weight_part(): pl.pallas_call(functools.partial(weight_kernel, first, last), in_specs=[p...  24.4 us
    pallas_call x2, Pallas kernels, input_part(): pl.pallas_call(input_kernel, in_specs=[pl.BlockSpec(memory_space=pltpu.SM...  17.6 us
    pallas_call x1, Pallas kernels, forward(): pl.pallas_call(forward_kernel, in_specs=[pl.BlockSpec(memory_space=pltpu....  12 us
    all_to_all x1, starting transfers between devices, per_device(): rows = lax.all_to_all(half(rows, 1, y) + arrived, 'sp', 0, 0)  6.47 us
    unnamed x42, local copies, waits for them, and re-layouts  3.83 us
    another operation x6, other arithmetic, in_order(): jnp.stack([jnp.where(bit == 0, own, other), jnp.where(bit == 0, other, ow...  3.69 us
  transfers between devices with their start and end apart: 27, of which 11 were waited for; matrix products, arithmetic and copies ran while one was open for 10% of the time, Pallas kernels for 34%

profile of v3, /device:TPU:0, one launch (start us, length us, event | category | flops | bytes accessed | tf_op | source)
XLA Modules:
  0.0 165.7 jit_solution(10618956802281211609)
XLA Ops:
  0.6 3.1 %collective-permute-start = (bf16[256,1024]{1,0:T(8,128)(2,1)}, bf16[256,1024]{1,0:T(8,128)(2,1)S(1)}, u32[]{:S(2)}, u32[]{:S(2)}) collective-permute-start(bf16[256,1024]{1,0:T(8,128)(2,1)} %bitcast.99), channel_id=1, source_target_pairs={{0,2},{1,3},{2,0},{3,1},{4,6},{5,7},{6,4},{7,5},{8,10},{9,11},{10,... | collective-permute-start | bytes 1572872 | tf_op jit(solution)/shard_map/ppermute | solution.py:481
  4.4 1.6 collective-permute-start.2
  6.0 9.9 %collective-permute-done.near_ref.refs_1_ = bf16[256,1024]{1,0:T(8,128)(2,1)S(1)} collective-permute-done((bf16[256,1024]{1,0:T(8,128)(2,1)}, bf16[256,1024]{1,0:T(8,128)(2,1)S(1)}, u32[]{:S(2)}, u32[]{:S(2)}) %collective-permute-start) | collective-permute-done | bytes 524320 | tf_op jit(solution)/shard_map/ppermute | solution.py:481
  15.9 2.2 %collective-permute-done.2.far_ref.refs_4_ = bf16[256,1024]{1,0:T(8,128)(2,1)S(1)} collective-permute-done((bf16[256,1024]{1,0:T(8,128)(2,1)}, bf16[256,1024]{1,0:T(8,128)(2,1)S(1)}, u32[]{:S(2)}, u32[]{:S(2)}) %collective-permute-start.2) | collective-permute-done | bytes 524320 | tf_op jit(solution)/shard_map/ppermute | solution.py:481
  18.8 1.3 collective-permute-start.4
  20.1 1.6 collective-permute-start.5
  22.2 2.0 %pick.1 = (bf16[7,32,256]{2,1,0:T(8,128)(2,1)}, bf16[7,32,256]{2,1,0:T(8,128)(2,1)}) custom-call(s32[2]{0:T(128)} %get-tuple-element.106.place_ref, bf16[27,32,512]{2,1,0:T(8,128)(2,1)} %weights_ref.1), custom_call_target="tpu_custom_call" | custom-call | tf_op jit(solution)/shard_map/pick/pallas_call | solution.py:393
  24.8 1.3 copy.18.refs_9_
  27.4 5.5 %weight_part.4.refs_0_ = f32[1792,256]{1,0:T(8,128)} custom-call(s32[3]{0:T(128)} %add_add_fusion.1.place_ref, bf16[64,8192]{1,0:T(8,128)(2,1)} %bitcast.93, bf16[256,1024]{1,0:T(8,128)(2,1)} %bitcast.102, bf16[256,1024]{1,0:T(8,128)(2,1)} %copy-done.11), custom_call_target="tpu_custom_call" | custom-call | flops 1811939328 | bytes 5242880 | tf_op jit(solution)/shard_map/weight_part/pallas_call | solution.py:276
  32.9 2.2 %collective-permute-done.6 = bf16[7,32,256]{2,1,0:T(8,128)(2,1)S(1)} collective-permute-done((bf16[7,32,256]{2,1,0:T(8,128)(2,1)}, bf16[7,32,256]{2,1,0:T(8,128)(2,1)S(1)}, u32[]{:S(2)}, u32[]{:S(2)}) %collective-permute-start.6) | collective-permute-done | bytes 114720 | tf_op jit(solution)/shard_map/ppermute | solution.py:481
  35.1 1.0 collective-permute-done.4
  36.1 1.3 collective-permute-start.7
  37.5 1.6 collective-permute-start.8
  39.1 4.4 %collective-permute-start.9 = (bf16[2,7,32,256]{3,2,1,0:T(8,128)(2,1)S(1)}, bf16[2,7,32,256]{3,2,1,0:T(8,128)(2,1)S(1)}, u32[]{:S(2)}, u32[]{:S(2)}) collective-permute-start(bf16[2,7,32,256]{3,2,1,0:T(8,128)(2,1)S(1)} %pad_maximum_fusion.4), channel_id=1, source_target_pairs={{0,2},{1,3},{2,4},{3,5},{4,6},{5,7},{6,0},{7,1},{8,10},{9,11},{10,... | collective-permute-start | bytes 688136 | tf_op jit(solution)/shard_map/ppermute | solution.py:481
  43.5 1.0 collective-permute-start.10
  44.4 2.8 %collective-permute-start.11 = (bf16[2,7,32,256]{3,2,1,0:T(8,128)(2,1)S(1)}, bf16[2,7,32,256]{3,2,1,0:T(8,128)(2,1)S(1)}, u32[]{:S(2)}, u32[]{:S(2)}) collective-permute-start(bf16[2,7,32,256]{3,2,1,0:T(8,128)(2,1)S(1)} %pad_maximum_fusion.4), channel_id=1, source_target_pairs={{0,6},{1,7},{2,0},{3,1},{4,2},{5,3},{6,4},{7,5},{8,14},{9,15},{10,... | collective-permute-start | bytes 688136 | tf_op jit(solution)/shard_map/ppermute | solution.py:481
  47.9 6.2 %weight_part.5.refs_0_ = f32[1792,256]{1,0:T(8,128)} custom-call(s32[3]{0:T(128)} %add_add_fusion.2.place_ref, bf16[64,8192]{1,0:T(8,128)(2,1)} %bitcast.94, bf16[256,1024]{1,0:T(8,128)(2,1)} %copy-done.10, bf16[256,1024]{1,0:T(8,128)(2,1)} %collective-permute-done.5.far_ref.refs_5_, f32[1792,256]{1,0:T(8,128)} %weight_part.4.refs_0_), custom_call_target="tpu_custom_call" | custom-call | flops 1811939328 | bytes 5242880 | tf_op jit(solution)/shard_map/weight_part/pallas_call | solution.py:276
  54.1 2.9 %collective-permute-done.10 = bf16[2,7,32,256]{3,2,1,0:T(8,128)(2,1)S(1)} collective-permute-done((bf16[2,7,32,256]{3,2,1,0:T(8,128)(2,1)S(1)}, bf16[2,7,32,256]{3,2,1,0:T(8,128)(2,1)S(1)}, u32[]{:S(2)}, u32[]{:S(2)}) %collective-permute-start.10) | collective-permute-done | bytes 229408 | tf_op jit(solution)/shard_map/ppermute | solution.py:481
  56.9 9.1 %collective-permute-done.11 = bf16[2,7,32,256]{3,2,1,0:T(8,128)(2,1)S(1)} collective-permute-done((bf16[2,7,32,256]{3,2,1,0:T(8,128)(2,1)S(1)}, bf16[2,7,32,256]{3,2,1,0:T(8,128)(2,1)S(1)}, u32[]{:S(2)}, u32[]{:S(2)}) %collective-permute-start.11) | collective-permute-done | bytes 229408 | tf_op jit(solution)/shard_map/ppermute | solution.py:481
  66.9 1.5 collective-permute-start.13
  68.5 1.6 collective-permute-start.12
  70.8 2.6 %collective-permute-start.15 = (bf16[64,2048]{1,0:T(8,128)(2,1)S(1)}, bf16[64,2048]{1,0:T(8,128)(2,1)S(1)}, u32[]{:S(2)}, u32[]{:S(2)}) collective-permute-start(bf16[64,2048]{1,0:T(8,128)(2,1)S(1)} %get-tuple-element.97), channel_id=1, source_target_pairs={{0,4},{1,5},{2,6},{3,7},{4,0},{5,1},{6,2},{7,3},{8,12},{9,13},{10,... | collective-permute-start | bytes 786440 | tf_op jit(solution)/shard_map/ppermute | solution.py:481
  73.4 1.2 collective-permute-start.16
  74.6 6.1 %weight_part.6.refs_0_ = f32[1792,256]{1,0:T(8,128)} custom-call(s32[3]{0:T(128)} %get-tuple-element.105.place_ref, bf16[64,8192]{1,0:T(8,128)(2,1)} %bitcast.95, bf16[256,1024]{1,0:T(8,128)(2,1)} %copy-done.5, bf16[256,1024]{1,0:T(8,128)(2,1)} %copy-done.12, f32[1792,256]{1,0:T(8,128)} %weight_part.5.refs_0_), custom_call_target="tpu_custom_call" | custom-call | flops 1811939328 | bytes 5242880 | tf_op jit(solution)/shard_map/weight_part/pallas_call | solution.py:276
  81.4 0.8 copy-done.13
  82.3 6.6 %weight_part.7 = (f32[8,16,1792]{2,1,0:T(8,128)}, f32[8,16,1792]{2,1,0:T(8,128)}) custom-call(s32[3]{0:T(128)} %get-tuple-element.104.place_ref, bf16[64,8192]{1,0:T(8,128)(2,1)} %bitcast.96, bf16[256,1024]{1,0:T(8,128)(2,1)} %copy-done.6, bf16[256,1024]{1,0:T(8,128)(2,1)} %copy-done.13, f32[1792,256]{1,0:T(8,128)} %weight_part.6.refs_0_), custom_call_target="tpu_custom_call" | custom-call | flops 1811939328 | bytes 5242880 | tf_op jit(solution)/shard_map/weight_part/pallas_call | solution.py:276
  88.8 2.4 %collective-permute-done.15 = bf16[64,2048]{1,0:T(8,128)(2,1)S(1)} collective-permute-done((bf16[64,2048]{1,0:T(8,128)(2,1)S(1)}, bf16[64,2048]{1,0:T(8,128)(2,1)S(1)}, u32[]{:S(2)}, u32[]{:S(2)}) %collective-permute-start.15) | collective-permute-done | bytes 262176 | tf_op jit(solution)/shard_map/ppermute | solution.py:481
  91.6 1.4 pad_maximum_fusion.own_ref
  94.8 1.1 fusion.4
  95.9 7.9 %collective-permute-start.19 = (bf16[256,1024]{1,0:T(8,128)(2,1)}, bf16[256,1024]{1,0:T(8,128)(2,1)}, u32[]{:S(2)}, u32[]{:S(2)}) collective-permute-start(bf16[256,1024]{1,0:T(8,128)(2,1)} %get-tuple-element.95), channel_id=1, source_target_pairs={{0,2},{1,3},{2,4},{3,5},{4,6},{5,7},{8,10},{9,11},{10,12},{11,13},... | collective-permute-start | bytes 1572872 | tf_op jit(solution)/shard_map/ppermute | solution.py:481
  103.8 1.3 collective-permute-start.20
  105.1 1.7 %collective-permute-done.18 = f32[8,8,1792]{2,1,0:T(8,128)S(1)} collective-permute-done((f32[8,8,1792]{2,1,0:T(8,128)S(1)}, f32[8,8,1792]{2,1,0:T(8,128)S(1)}, u32[]{:S(2)}, u32[]{:S(2)}) %collective-permute-start.18) | collective-permute-done | bytes 458784 | tf_op jit(solution)/shard_map/ppermute | solution.py:481
  106.7 0.8 bitcast_add_fusion
  107.6 6.5 %all-to-all-start = ((f32[8,8,1792]{2,1,0:T(8,128)}), f32[8,8,1792]{2,1,0:T(8,128)S(1)}, u32[]{:S(2)}, u32[]{:S(2)}) async-start(f32[8,8,1792]{2,1,0:T(8,128)} %bitcast_add_fusion), calls=%async_computation | async-start | bytes 917504 | tf_op jit(solution)/shard_map/all_to_all | solution.py:545
  114.0 2.0 %select_bitcast_fusion.1 = (bf16[1,2,4,2,7,32,64]{6,5,4,3,2,1,0:T(8,128)(2,1)S(1)}, bf16[1,2,4,2,7,32,64]{6,5,4,3,2,1,0:T(8,128)(2,1)S(1)}) fusion(pred[]{:T(512)S(6)} %eq.31, bf16[2,4,2,7,32,256]{5,4,3,2,1,0:T(8,128)(2,1)} %collective-permute-done.21.other_ref, s32[]{:T(128)S(6)} %select_n.159, bf16[1,4,2,7,32,256]{5,4,3,2,1,0:T(8,128)(2,1)S(1)} %get-tuple-element.93, ...), kind=kLoop, calls=%fused_computation.8 | loop fusion | flops 2293760 | bytes 3211269 | tf_op jit(solution)/shard_map/stack | solution.py:438
  117.6 0.9 copy.15
  118.4 0.7 copy.16
  119.1 3.4 %collective-permute-done.20.above_ref = bf16[256,1024]{1,0:T(8,128)(2,1)} collective-permute-done((bf16[256,1024]{1,0:T(8,128)(2,1)}, bf16[256,1024]{1,0:T(8,128)(2,1)}, u32[]{:S(2)}, u32[]{:S(2)}) %collective-permute-start.20) | collective-permute-done | bytes 524320 | tf_op jit(solution)/shard_map/ppermute | solution.py:481
  122.6 8.8 %input_part.2 = (f32[128,1024]{1,0:T(8,128)}, f32[128,1024]{1,0:T(8,128)}) custom-call(s32[2]{0:T(128)} %get-tuple-element.107.place_ref, bf16[256,1024]{1,0:T(8,128)(2,1)} %collective-permute-done.19.below_ref, bf16[256,2048]{1,0:T(8,128)(2,1)} %bitcast.88, bf16[256,1024]{1,0:T(8,128)(2,1)} %collective-permute-done.20.above_ref, ...), custom_call_target="tpu_custom_call" | custom-call | flops 3623878656 | bytes 8388608 | tf_op jit(solution)/shard_map/input_part/pallas_call | solution.py:344
  131.9 1.3 copy.17.refs_8_
  133.2 12.0 %forward.1 = bf16[64,8192]{1,0:T(8,128)(2,1)} custom-call(s32[8]{0:T(128)} %stack.195.place_ref, bf16[256,1024]{1,0:T(8,128)(2,1)} %bitcast.103, bf16[256,1024]{1,0:T(8,128)(2,1)} %copy-done.10, bf16[256,1024]{1,0:T(8,128)(2,1)} %copy-done.5, bf16[256,1024]{1,0:T(8,128)(2,1)} %copy-done.6, bf16[256,1024]{1,0:T(8,128)(2,1)} %copy-done.11, ...), custom_call_target="tpu_custom_call" | custom-call | flops 7247757312 | bytes 6291456 | tf_op jit(solution)/shard_map/forward/pallas_call | solution.py:186
  145.2 1.6 collective-permute-start.24
  146.8 1.5 collective-permute-start.23
  149.6 8.8 %input_part.3 = (f32[128,1024]{1,0:T(8,128)}, f32[128,1024]{1,0:T(8,128)}) custom-call(s32[2]{0:T(128)} %pad_add_fusion.2.place_ref, bf16[256,1024]{1,0:T(8,128)(2,1)} %collective-permute-done.19.below_ref, bf16[256,2048]{1,0:T(8,128)(2,1)} %bitcast.89, bf16[256,1024]{1,0:T(8,128)(2,1)} %collective-permute-done.20.above_ref, ...), custom_call_target="tpu_custom_call" | custom-call | flops 3623878656 | bytes 8388608 | tf_op jit(solution)/shard_map/input_part/pallas_call | solution.py:344
  158.7 0.8 copy-done.8
  160.0 0.8 pad_maximum_fusion.3
  161.4 0.9 copy-done.4
  162.4 3.3 %arrange.1 = f32[27,32,512]{2,1,0:T(8,128)} custom-call(f32[1]{0:T(128)} %copy.33.scale_ref, s32[1]{0:T(128)} %bitcast.2.core_ref, f32[2,8,8,1792]{3,2,1,0:T(8,128)} %copy-done.1, f32[2,8,8,1792]{3,2,1,0:T(8,128)} %copy-done.4), custom_call_target="tpu_custom_call" | custom-call | tf_op jit(solution)/shard_map/arrange/pallas_call | solution.py:423
  (95 shorter events, 12.7 us)
Async XLA Ops:
  0.6 15.2 %collective-permute-start = (bf16[256,1024]{1,0:T(8,128)(2,1)}, bf16[256,1024]{1,0:T(8,128)(2,1)S(1)}, u32[]{:S(2)}, u32[]{:S(2)}) collective-permute-start(bf16[256,1024]{1,0:T(8,128)(2,1)} %bitcast.99), channel_id=1, source_target_pairs={{0,2},{1,3},{2,0},{3,1},{4,6},{5,7},{6,4},{7,5},{8,10},{9,11},{10,... | collective-permute-start | bytes 1572872 | tf_op jit(solution)/shard_map/ppermute | solution.py:481
  3.7 12.1 %collective-permute-start.1 = (bf16[256,1024]{1,0:T(8,128)(2,1)}, bf16[256,1024]{1,0:T(8,128)(2,1)S(1)}, u32[]{:S(2)}, u32[]{:S(2)}) collective-permute-start(bf16[256,1024]{1,0:T(8,128)(2,1)} %bitcast.100), channel_id=1, source_target_pairs={{2,4},{3,5},{4,2},{5,3},{10,12},{11,13},{12,10},{13,11},{18,20},{1... | collective-permute-start | bytes 1572872 | tf_op jit(solution)/shard_map/ppermute | solution.py:481
  4.4 13.7 %collective-permute-start.2 = (bf16[256,1024]{1,0:T(8,128)(2,1)}, bf16[256,1024]{1,0:T(8,128)(2,1)S(1)}, u32[]{:S(2)}, u32[]{:S(2)}) collective-permute-start(bf16[256,1024]{1,0:T(8,128)(2,1)} %bitcast.101), channel_id=1, source_target_pairs={{0,1},{1,0},{2,3},{3,2},{4,5},{5,4},{6,7},{7,6},{8,9},{9,8},{10,11... | collective-permute-start | bytes 1572872 | tf_op jit(solution)/shard_map/ppermute | solution.py:481
  15.9 17.0 %copy-start.10 = (bf16[256,1024]{1,0:T(8,128)(2,1)}, bf16[256,1024]{1,0:T(8,128)(2,1)S(1)}, u32[]{:S(2)}) copy-start(bf16[256,1024]{1,0:T(8,128)(2,1)S(1)} %collective-permute-done.near_ref.refs_1_) | copy-start | bytes 1572868
  18.1 9.3 %copy-start.11 = (bf16[256,1024]{1,0:T(8,128)(2,1)}, bf16[256,1024]{1,0:T(8,128)(2,1)S(1)}, u32[]{:S(2)}) copy-start(bf16[256,1024]{1,0:T(8,128)(2,1)S(1)} %collective-permute-done.2.far_ref.refs_4_) | copy-start | bytes 1572868
  18.1 17.0 %collective-permute-start.3 = (bf16[256,1024]{1,0:T(8,128)(2,1)S(1)}, bf16[256,1024]{1,0:T(8,128)(2,1)S(1)}, u32[]{:S(2)}, u32[]{:S(2)}) collective-permute-start(bf16[256,1024]{1,0:T(8,128)(2,1)S(1)} %collective-permute-done.near_ref.refs_1_), channel_id=1, source_target_pairs={{2,4},{3,5},{4,2},{5,3},{10,12},{11,13},{12,10},{13,11},{18,20},{1... | collective-permute-start | bytes 1572872 | tf_op jit(solution)/shard_map/ppermute | solution.py:481
  18.8 17.3 %collective-permute-start.4 = (bf16[256,1024]{1,0:T(8,128)(2,1)S(1)}, bf16[256,1024]{1,0:T(8,128)(2,1)S(1)}, u32[]{:S(2)}, u32[]{:S(2)}) collective-permute-start(bf16[256,1024]{1,0:T(8,128)(2,1)S(1)} %collective-permute-done.1), channel_id=1, source_target_pairs={{2,0},{3,1},{4,6},{5,7},{10,8},{11,9},{12,14},{13,15},{18,16},{19,... | collective-permute-start | bytes 1572872 | tf_op jit(solution)/shard_map/ppermute | solution.py:481
  20.1 16.0 %collective-permute-start.5 = (bf16[256,1024]{1,0:T(8,128)(2,1)S(1)}, bf16[256,1024]{1,0:T(8,128)(2,1)}, u32[]{:S(2)}, u32[]{:S(2)}) collective-permute-start(bf16[256,1024]{1,0:T(8,128)(2,1)S(1)} %collective-permute-done.near_ref.refs_1_), channel_id=1, source_target_pairs={{0,1},{1,0},{2,3},{3,2},{4,5},{5,4},{6,7},{7,6},{8,9},{9,8},{10,11... | collective-permute-start | bytes 1572872 | tf_op jit(solution)/shard_map/ppermute | solution.py:481
  24.2 10.8 %collective-permute-start.6 = (bf16[7,32,256]{2,1,0:T(8,128)(2,1)}, bf16[7,32,256]{2,1,0:T(8,128)(2,1)S(1)}, u32[]{:S(2)}, u32[]{:S(2)}) collective-permute-start(bf16[7,32,256]{2,1,0:T(8,128)(2,1)} %get-tuple-element.50), channel_id=1, source_target_pairs={{0,1},{1,0},{2,3},{3,2},{4,5},{5,4},{6,7},{7,6},{8,9},{9,8},{10,11... | collective-permute-start | bytes 344072 | tf_op jit(solution)/shard_map/ppermute | solution.py:481
  27.4 11.7 %copy-start.9 = (bf16[7,32,256]{2,1,0:T(8,128)(2,1)S(1)}, bf16[7,32,256]{2,1,0:T(8,128)(2,1)}, u32[]{:S(2)}) copy-start(bf16[7,32,256]{2,1,0:T(8,128)(2,1)} %get-tuple-element.55) | copy-start | bytes 344068
  36.1 30.0 %collective-permute-start.7 = (bf16[256,1024]{1,0:T(8,128)(2,1)S(1)}, bf16[256,1024]{1,0:T(8,128)(2,1)S(1)}, u32[]{:S(2)}, u32[]{:S(2)}) collective-permute-start(bf16[256,1024]{1,0:T(8,128)(2,1)S(1)} %collective-permute-done.3), channel_id=1, source_target_pairs={{2,0},{3,1},{4,6},{5,7},{10,8},{11,9},{12,14},{13,15},{18,16},{19,... | collective-permute-start | bytes 1572872 | tf_op jit(solution)/shard_map/ppermute | solution.py:481
  37.4 16.6 %copy-start.5 = (bf16[256,1024]{1,0:T(8,128)(2,1)}, bf16[256,1024]{1,0:T(8,128)(2,1)S(1)}, u32[]{:S(2)}) copy-start(bf16[256,1024]{1,0:T(8,128)(2,1)S(1)} %broadcast_select_fusion.1.near_ref.refs_2_) | copy-start | bytes 1572868
  37.5 28.6 %collective-permute-start.8 = (bf16[256,1024]{1,0:T(8,128)(2,1)S(1)}, bf16[256,1024]{1,0:T(8,128)(2,1)S(1)}, u32[]{:S(2)}, u32[]{:S(2)}) collective-permute-start(bf16[256,1024]{1,0:T(8,128)(2,1)S(1)} %broadcast_select_fusion.1.near_ref.refs_2_), channel_id=1, source_target_pairs={{0,1},{1,0},{2,3},{3,2},{4,5},{5,4},{6,7},{7,6},{8,9},{9,8},{10,11... | collective-permute-start | bytes 1572872 | tf_op jit(solution)/shard_map/ppermute | solution.py:481
  39.1 15.0 %collective-permute-start.9 = (bf16[2,7,32,256]{3,2,1,0:T(8,128)(2,1)S(1)}, bf16[2,7,32,256]{3,2,1,0:T(8,128)(2,1)S(1)}, u32[]{:S(2)}, u32[]{:S(2)}) collective-permute-start(bf16[2,7,32,256]{3,2,1,0:T(8,128)(2,1)S(1)} %pad_maximum_fusion.4), channel_id=1, source_target_pairs={{0,2},{1,3},{2,4},{3,5},{4,6},{5,7},{6,0},{7,1},{8,10},{9,11},{10,... | collective-permute-start | bytes 688136 | tf_op jit(solution)/shard_map/ppermute | solution.py:481
  43.5 13.4 %collective-permute-start.10 = (bf16[2,7,32,256]{3,2,1,0:T(8,128)(2,1)S(1)}, bf16[2,7,32,256]{3,2,1,0:T(8,128)(2,1)S(1)}, u32[]{:S(2)}, u32[]{:S(2)}) collective-permute-start(bf16[2,7,32,256]{3,2,1,0:T(8,128)(2,1)S(1)} %pad_maximum_fusion.4), channel_id=1, source_target_pairs={{0,4},{1,5},{2,6},{3,7},{4,0},{5,1},{6,2},{7,3},{8,12},{9,13},{10,... | collective-permute-start | bytes 688136 | tf_op jit(solution)/shard_map/ppermute | solution.py:481
  44.4 21.6 %collective-permute-start.11 = (bf16[2,7,32,256]{3,2,1,0:T(8,128)(2,1)S(1)}, bf16[2,7,32,256]{3,2,1,0:T(8,128)(2,1)S(1)}, u32[]{:S(2)}, u32[]{:S(2)}) collective-permute-start(bf16[2,7,32,256]{3,2,1,0:T(8,128)(2,1)S(1)} %pad_maximum_fusion.4), channel_id=1, source_target_pairs={{0,6},{1,7},{2,0},{3,1},{4,2},{5,3},{6,4},{7,5},{8,14},{9,15},{10,... | collective-permute-start | bytes 688136 | tf_op jit(solution)/shard_map/ppermute | solution.py:481
  66.1 0.8 copy-start.12
  66.2 4.4 %copy-start.2 = (bf16[1,64,8192]{2,1,0:T(8,128)(2,1)S(1)}, bf16[1,64,8192]{2,1,0:T(8,128)(2,1)}, u32[]{:S(2)}) copy-start(bf16[1,64,8192]{2,1,0:T(8,128)(2,1)} %param.8) | copy-start | bytes 3145732
  66.9 24.4 %collective-permute-start.13 = (bf16[4,2,7,32,256]{4,3,2,1,0:T(8,128)(2,1)S(1)}, bf16[4,2,7,32,256]{4,3,2,1,0:T(8,128)(2,1)S(1)}, u32[]{:S(2)}, u32[]{:S(2)}) collective-permute-start(bf16[4,2,7,32,256]{4,3,2,1,0:T(8,128)(2,1)S(1)} %constant_dynamic-slice_fusion.5), channel_id=1, source_target_pairs={{0,16},{8,24},{16,0},{24,8},{1,17},{9,25},{17,1},{25,9},{2,18},{10... | collective-permute-start | bytes 2752520 | tf_op jit(solution)/shard_map/ppermute | solution.py:481
  68.5 12.3 %copy-start.6 = (bf16[256,1024]{1,0:T(8,128)(2,1)}, bf16[256,1024]{1,0:T(8,128)(2,1)S(1)}, u32[]{:S(2)}) copy-start(bf16[256,1024]{1,0:T(8,128)(2,1)S(1)} %broadcast_select_fusion.near_ref.refs_3_) | copy-start | bytes 1572868
  68.5 12.9 %collective-permute-start.12 = (bf16[256,1024]{1,0:T(8,128)(2,1)S(1)}, bf16[256,1024]{1,0:T(8,128)(2,1)S(1)}, u32[]{:S(2)}, u32[]{:S(2)}) collective-permute-start(bf16[256,1024]{1,0:T(8,128)(2,1)S(1)} %broadcast_select_fusion.near_ref.refs_3_), channel_id=1, source_target_pairs={{0,1},{1,0},{2,3},{3,2},{4,5},{5,4},{6,7},{7,6},{8,9},{9,8},{10,11... | collective-permute-start | bytes 1572872 | tf_op jit(solution)/shard_map/ppermute | solution.py:481
  70.8 18.1 %collective-permute-start.14 = (bf16[64,2048]{1,0:T(8,128)(2,1)S(1)}, bf16[64,2048]{1,0:T(8,128)(2,1)S(1)}, u32[]{:S(2)}, u32[]{:S(2)}) collective-permute-start(bf16[64,2048]{1,0:T(8,128)(2,1)S(1)} %get-tuple-element.98), channel_id=1, source_target_pairs={{0,2},{1,3},{2,4},{3,5},{4,6},{5,7},{6,0},{7,1},{8,10},{9,11},{10,... | collective-permute-start | bytes 786440 | tf_op jit(solution)/shard_map/ppermute | solution.py:481
  70.8 20.4 %collective-permute-start.15 = (bf16[64,2048]{1,0:T(8,128)(2,1)S(1)}, bf16[64,2048]{1,0:T(8,128)(2,1)S(1)}, u32[]{:S(2)}, u32[]{:S(2)}) collective-permute-start(bf16[64,2048]{1,0:T(8,128)(2,1)S(1)} %get-tuple-element.97), channel_id=1, source_target_pairs={{0,4},{1,5},{2,6},{3,7},{4,0},{5,1},{6,2},{7,3},{8,12},{9,13},{10,... | collective-permute-start | bytes 786440 | tf_op jit(solution)/shard_map/ppermute | solution.py:481
  73.4 17.8 %collective-permute-start.16 = (bf16[64,2048]{1,0:T(8,128)(2,1)S(1)}, bf16[64,2048]{1,0:T(8,128)(2,1)S(1)}, u32[]{:S(2)}, u32[]{:S(2)}) collective-permute-start(bf16[64,2048]{1,0:T(8,128)(2,1)S(1)} %get-tuple-element.96), channel_id=1, source_target_pairs={{0,6},{1,7},{2,0},{3,1},{4,2},{5,3},{6,4},{7,5},{8,14},{9,15},{10,... | collective-permute-start | bytes 786440 | tf_op jit(solution)/shard_map/ppermute | solution.py:481
  81.4 0.8 copy-start.13
  91.3 2.7 %collective-permute-start.17 = (f32[8,16,1792]{2,1,0:T(8,128)}, f32[8,16,1792]{2,1,0:T(8,128)S(1)}, u32[]{:S(2)}, u32[]{:S(2)}) collective-permute-start(f32[8,16,1792]{2,1,0:T(8,128)} %get-tuple-element.68), channel_id=1, source_target_pairs={{0,8},{8,0},{16,24},{24,16},{1,9},{9,1},{17,25},{25,17},{2,10},{10... | collective-permute-start | bytes 2752520 | tf_op jit(solution)/shard_map/ppermute | solution.py:481
  91.5 2.4 %copy-start.3 = (f32[8,16,1792]{2,1,0:T(8,128)S(1)}, f32[8,16,1792]{2,1,0:T(8,128)}, u32[]{:S(2)}) copy-start(f32[8,16,1792]{2,1,0:T(8,128)} %get-tuple-element.67) | copy-start | bytes 2752516
  93.0 21.0 %collective-permute-start.21 = (bf16[2,4,2,7,32,256]{5,4,3,2,1,0:T(8,128)(2,1)}, bf16[2,4,2,7,32,256]{5,4,3,2,1,0:T(8,128)(2,1)}, u32[]{:S(2)}, u32[]{:S(2)}) collective-permute-start(bf16[2,4,2,7,32,256]{5,4,3,2,1,0:T(8,128)(2,1)} %pad_maximum_fusion.own_ref), channel_id=1, source_target_pairs={{0,8},{8,0},{16,24},{24,16},{1,9},{9,1},{17,25},{25,17},{2,10},{10... | collective-permute-start | bytes 5505032 | tf_op jit(solution)/shard_map/ppermute | solution.py:481
  94.1 12.6 %collective-permute-start.18 = (f32[8,8,1792]{2,1,0:T(8,128)S(1)}, f32[8,8,1792]{2,1,0:T(8,128)S(1)}, u32[]{:S(2)}, u32[]{:S(2)}) collective-permute-start(f32[8,8,1792]{2,1,0:T(8,128)S(1)} %dynamic-slice_bitcast_fusion), channel_id=1, source_target_pairs={{0,16},{8,24},{16,0},{24,8},{1,17},{9,25},{17,1},{25,9},{2,18},{10... | collective-permute-start | bytes 1376264 | tf_op jit(solution)/shard_map/ppermute | solution.py:481
  94.7 12.8 %copy-start = (bf16[4,64,2048]{2,1,0:T(8,128)(2,1)}, bf16[4,64,2048]{2,1,0:T(8,128)(2,1)S(1)}, u32[]{:S(2)}) copy-start(bf16[4,64,2048]{2,1,0:T(8,128)(2,1)S(1)} %constant_dynamic-slice_fusion) | copy-start | bytes 3145732
  95.9 23.2 %collective-permute-start.19 = (bf16[256,1024]{1,0:T(8,128)(2,1)}, bf16[256,1024]{1,0:T(8,128)(2,1)}, u32[]{:S(2)}, u32[]{:S(2)}) collective-permute-start(bf16[256,1024]{1,0:T(8,128)(2,1)} %get-tuple-element.95), channel_id=1, source_target_pairs={{0,2},{1,3},{2,4},{3,5},{4,6},{5,7},{8,10},{9,11},{10,12},{11,13},... | collective-permute-start | bytes 1572872 | tf_op jit(solution)/shard_map/ppermute | solution.py:481
  103.8 18.8 %collective-permute-start.20 = (bf16[256,1024]{1,0:T(8,128)(2,1)}, bf16[256,1024]{1,0:T(8,128)(2,1)}, u32[]{:S(2)}, u32[]{:S(2)}) collective-permute-start(bf16[256,1024]{1,0:T(8,128)(2,1)} %get-tuple-element.94), channel_id=1, source_target_pairs={{2,0},{3,1},{4,2},{5,3},{6,4},{7,5},{10,8},{11,9},{12,10},{13,11},... | collective-permute-start | bytes 1572872 | tf_op jit(solution)/shard_map/ppermute | solution.py:481
  107.6 37.7 %all-to-all-start = ((f32[8,8,1792]{2,1,0:T(8,128)}), f32[8,8,1792]{2,1,0:T(8,128)S(1)}, u32[]{:S(2)}, u32[]{:S(2)}) async-start(f32[8,8,1792]{2,1,0:T(8,128)} %bitcast_add_fusion), calls=%async_computation | async-start | bytes 917504 | tf_op jit(solution)/shard_map/all_to_all | solution.py:545
  131.3 13.9 %collective-permute-start.22 = (f32[128,1024]{1,0:T(8,128)}, f32[128,1024]{1,0:T(8,128)S(1)}, u32[]{:S(2)}, u32[]{:S(2)}) collective-permute-start(f32[128,1024]{1,0:T(8,128)} %get-tuple-element.77), channel_id=1, source_target_pairs={{0,1},{1,0},{2,3},{3,2},{4,5},{5,4},{6,7},{7,6},{8,9},{9,8},{10,11... | collective-permute-start | bytes 1572872 | tf_op jit(solution)/shard_map/ppermute | solution.py:481
  133.2 12.0 %copy-start.14 = (f32[128,1024]{1,0:T(8,128)S(1)}, f32[128,1024]{1,0:T(8,128)}, u32[]{:S(2)}) copy-start(f32[128,1024]{1,0:T(8,128)} %get-tuple-element.82) | copy-start | bytes 1572868
  145.2 13.1 %collective-permute-start.24 = (f32[128,1024]{1,0:T(8,128)S(1)}, f32[128,1024]{1,0:T(8,128)S(1)}, u32[]{:S(2)}, u32[]{:S(2)}) collective-permute-start(f32[128,1024]{1,0:T(8,128)S(1)} %copy-done.14), channel_id=1, source_target_pairs={{0,1},{1,0},{2,3},{3,2},{4,5},{5,4},{6,7},{7,6},{8,9},{9,8},{10,11... | collective-permute-start | bytes 1572872 | tf_op jit(solution)/shard_map/ppermute | solution.py:481
  146.8 11.5 %collective-permute-start.23 = (f32[8,8,1792]{2,1,0:T(8,128)S(1)}, f32[8,8,1792]{2,1,0:T(8,128)S(1)}, u32[]{:S(2)}, u32[]{:S(2)}) collective-permute-start(f32[8,8,1792]{2,1,0:T(8,128)S(1)} %all-to-all-done), channel_id=1, source_target_pairs={{0,16},{8,24},{16,0},{24,8},{1,17},{9,25},{17,1},{25,9},{2,18},{10... | collective-permute-start | bytes 1376264 | tf_op jit(solution)/shard_map/ppermute | solution.py:481
  158.4 1.0 copy-start.8
  158.5 1.5 copy-start.7
  158.6 2.3 %copy-start.1 = (f32[2,8,8,1792]{3,2,1,0:T(8,128)}, f32[2,8,8,1792]{3,2,1,0:T(8,128)S(1)}, u32[]{:S(2)}) copy-start(f32[2,8,8,1792]{3,2,1,0:T(8,128)S(1)} %pad_maximum_fusion.2.own_ref) | copy-start | bytes 2752516
  158.6 2.9 %collective-permute-start.25 = (f32[2,8,8,1792]{3,2,1,0:T(8,128)S(1)}, f32[2,8,8,1792]{3,2,1,0:T(8,128)S(1)}, u32[]{:S(2)}, u32[]{:S(2)}) collective-permute-start(f32[2,8,8,1792]{3,2,1,0:T(8,128)S(1)} %pad_maximum_fusion.2.own_ref), channel_id=1, source_target_pairs={{0,8},{8,0},{16,24},{24,16},{1,9},{9,1},{17,25},{25,17},{2,10},{10... | collective-permute-start | bytes 2752520 | tf_op jit(solution)/shard_map/ppermute | solution.py:481
  161.4 0.9 copy-start.4
